TPU v7x, 32 devices: a whole 2x2x4 slice. The times are simulated.
32 devices in a mesh: dp: 4 (over y, core), row: 2 (over x), col: 4 (over z).
Axes of the slice: x: 2, y: 2, z: 4, core: 2. Of those that a mesh axis runs over, the one named last changes fastest.
Arguments:
- inputs: bfloat16 [6144, 1024], P(('dp', 'row'), 'col'), may hold values from -14 to 14
- cotangent: bfloat16 [6144, 1024], P(('dp', 'row'), 'col'), may hold values from -20 to 20
- routes: int32 [6144, 8], P('dp'), may hold values from 0 to 31, all different within a row; in each aligned block of 1536 rows (0 to 1535, 1536 to 3071, ...) at most 480 rows name the same one
- gate_probs: float32 [6144, 8], P('dp'), may hold values from 0.06 to 0.2
- seq_ids: int32 [6144], P('dp'), may hold values from 0 to 2, as said below
- norm_gains: float32 [2, 1024], P(None, 'col'), may hold values from 0.5 to 1.5
- gain_moment: float32 [2, 1024], P(None, 'col'), may hold values from -112 to 112
- gain_second: float32 [2, 1024], P(None, 'col'), may hold values from 1290.24 to 5160.96
- query_weight: float32 [1024, 1024], P('col', 'row'), may hold values from -0.1875 to 0.1875
- query_moment: float32 [1024, 1024], P('col', 'row'), may hold values from -112 to 112
- query_second: float32 [1024, 1024], P('col', 'row'), may hold values from 1300.48 to 5222.4
- key_value_matrix: float32 [2, 1024, 512], P(None, 'col', 'row'), may hold values from -0.1875 to 0.1875
- key_value_first_moment: float32 [2, 1024, 512], P(None, 'col', 'row'), may hold values from -112 to 112
- key_value_second_moment: float32 [2, 1024, 512], P(None, 'col', 'row'), may hold values from 1300.48 to 5222.4
- out_weight: float32 [1024, 1024], P('row', 'col'), may hold values from -3 to 3
- out_moment: float32 [1024, 1024], P('row', 'col'), may hold values from -7 to 7
- out_second: float32 [1024, 1024], P('row', 'col'), may hold values from 5.08 to 20.4
- gate_up_weight: float32 [32, 1024, 2, 512], P('dp', 'col', None, 'row'), may hold values from -0.1875 to 0.1875
- gate_up_moment: float32 [32, 1024, 2, 512], P('dp', 'col', None, 'row'), may hold values from -20 to 20
- gate_up_second: float32 [32, 1024, 2, 512], P('dp', 'col', None, 'row'), may hold values from 50.9952 to 202.752
- down_weight: float32 [32, 512, 1024], P('dp', 'row', 'col'), may hold values from -1 to 1
- down_moment: float32 [32, 512, 1024], P('dp', 'row', 'col'), may hold values from -4 to 4
- down_second: float32 [32, 512, 1024], P('dp', 'row', 'col'), may hold values from 2.08896 to 8.2944
Outputs:
- block_output: bfloat16 [6144, 1024], P(('dp', 'row'), 'col')
- input_grad: float32 [6144, 1024], P(('dp', 'row'), 'col')
- gain_moment_new: float32 [2, 1024], P(None, 'col')
- gain_second_new: float32 [2, 1024], P(None, 'col')
- gains_new: float32 [2, 1024], P(None, 'col')
- query_moment_new: float32 [1024, 1024], P('col', 'row')
- query_second_new: float32 [1024, 1024], P('col', 'row')
- query_new: float32 [1024, 1024], P('col', 'row')
- key_value_moment_new: float32 [2, 1024, 512], P(None, 'col', 'row')
- key_value_second_new: float32 [2, 1024, 512], P(None, 'col', 'row')
- key_value_new: float32 [2, 1024, 512], P(None, 'col', 'row')
- out_moment_new: float32 [1024, 1024], P('row', 'col')
- out_second_new: float32 [1024, 1024], P('row', 'col')
- out_new: float32 [1024, 1024], P('row', 'col')
- gate_up_moment_new: float32 [32, 1024, 2, 512], P('dp', 'col', None, 'row')
- gate_up_second_new: float32 [32, 1024, 2, 512], P('dp', 'col', None, 'row')
- gate_up_new: float32 [32, 1024, 2, 512], P('dp', 'col', None, 'row')
- down_moment_new: float32 [32, 512, 1024], P('dp', 'row', 'col')
- down_second_new: float32 [32, 512, 1024], P('dp', 'row', 'col')
- down_new: float32 [32, 512, 1024], P('dp', 'row', 'col')
Inputs may be any that keep to these rules, and one draw needn't show every extreme that they name: `routes`: each row names 8 different experts; in each aligned block of 1536 rows (one replica) no expert is named by more than 480 rows, a bound that some block reaches. `seq_ids`: in each aligned block of 1536 tokens the numbers never fall, start at 0 and end at 2; sequence 1 begins within the block's first quarter and ends within its last quarter.
All inputs are finite; a program needn't handle non-finite values.
Results may differ from a plain program's by a relative error of at most 0.013.
The roundings to bfloat16 on the way count: a program that leaves them out, or rounds other values in their place, can miss the bound.
Values may be sent and summed in bfloat16 or wider, within the bound.
A program may use at most 256 MiB of HBM per device.

v0:
```python
import jax
import jax.numpy as jnp
from jax import lax
from jax.sharding import PartitionSpec as P

MODEL_WIDTH = 1024
QUERY_HEADS = 16
KEY_VALUE_HEADS = 8
HEAD_SIZE = 64
FF = 512
EXPERTS = 32
TOP = 8
STEP = 10


norm_epsilon = 1e-06
first_decay = 0.9
second_decay = 0.95
adam_epsilon = 1e-08
weight_decay = 0.1
masked_score = -1e30
expert_block = 8


def shortened(value):
    return jax.tree.map(lambda a: a.astype(jnp.bfloat16) if a.dtype == jnp.float32 else a, value)


def feature_total(row_values):
    return lax.psum(row_values, "col")


def rms_scale(value_rows):
    squares = feature_total(jnp.sum(value_rows * value_rows, axis=1))
    return lax.rsqrt(squares / MODEL_WIDTH + norm_epsilon)[:, None]


def norm_back(grad_normed, value_rows, scale, gain):
    inner = feature_total(jnp.sum(grad_normed * gain * value_rows, axis=1))[:, None]
    grad_values = scale * gain * grad_normed - value_rows * scale**3 * inner / MODEL_WIDTH
    grad_gain = jnp.sum(grad_normed * value_rows * scale, axis=0)
    return (grad_values, grad_gain)


def gather_rows(value_rows):
    return lax.all_gather(value_rows, "row", axis=0, tiled=True)


def reduce_rows(value_rows):
    return lax.psum_scatter(value_rows, "row", scatter_dimension=0, tiled=True)


def gather_cols(value_rows):
    return jax.tree.map(
        lambda part, own: part.astype(own.dtype),
        lax.all_gather(shortened(value_rows), "col", axis=0, tiled=True),
        value_rows,
    )


def reduce_cols(value_rows):
    return lax.psum_scatter(value_rows, "col", scatter_dimension=0, tiled=True)


def reduce_slots(term_fn, slot_rows):
    return lax.psum_scatter(
        term_fn(jnp.int32(0), slot_rows * lax.axis_size("col")),
        "col",
        scatter_dimension=0,
        tiled=True,
    )


def fold_slots(value_rows, fold_fn, initial):
    return fold_fn(initial, lax.all_gather(value_rows, "col", axis=0, tiled=True), jnp.int32(0))


def dispatch(route_rows, prob_rows, capacity, rep_tokens):
    flat_routes = route_rows.reshape(-1)
    entries = flat_routes.shape[0]
    sorted_order = jnp.argsort(flat_routes, stable=True)
    expert_ids = jnp.arange(EXPERTS, dtype=jnp.int32)
    counts = jnp.sum((flat_routes[:, None] == expert_ids[None, :]).astype(jnp.int32), axis=0)
    offsets = jnp.cumsum(counts) - counts
    slot_index = jnp.arange(capacity, dtype=jnp.int32)[:, None]
    position = jnp.minimum(offsets[None, :] + slot_index, entries - 1)
    source = sorted_order[position]
    filled = slot_index < counts[None, :]
    tokens = jnp.where(filled, source // TOP, rep_tokens)
    weights = jnp.where(filled, prob_rows.reshape(-1)[source], 0.0)
    return (tokens, weights)


def adam_update(weight, moment, second, gradient, step_rate, decay_rate):
    moment_new = first_decay * moment + (1.0 - first_decay) * gradient
    second_new = second_decay * second + (1.0 - second_decay) * gradient * gradient
    step_size = step_rate / (1.0 - first_decay**STEP)
    denominator = jnp.sqrt(second_new / (1.0 - second_decay**STEP)) + adam_epsilon
    weight_new = weight - step_size * moment_new / denominator - step_rate * decay_rate * weight
    return (moment_new, second_new, weight_new)


def per_device(
    inputs,
    cotangent,
    routes,
    gate_probs,
    seq_ids,
    norm_gains,
    gain_moment,
    gain_second,
    query_weight,
    query_moment,
    query_second,
    key_value_matrix,
    key_value_first_moment,
    key_value_second_moment,
    out_weight,
    out_moment,
    out_second,
    gate_up_weight,
    gate_up_moment,
    gate_up_second,
    down_weight,
    down_moment,
    down_second,
):
    rep_tokens = routes.shape[0]
    col_count = lax.axis_size("col")
    col_rows = rep_tokens // col_count
    width_part = inputs.shape[1]
    query_width = query_weight.shape[1]
    key_width = key_value_matrix.shape[2]
    group_width = QUERY_HEADS // KEY_VALUE_HEADS
    scale_factor = HEAD_SIZE ** (-0.5)
    capacity = rep_tokens * TOP // EXPERTS * 5 // 4
    slot_rows = capacity // col_count
    heads_here = key_width // HEAD_SIZE
    residual = inputs.astype(jnp.float32)
    first_scale = rms_scale(residual)
    normed = (residual * first_scale * norm_gains[0]).astype(jnp.bfloat16)
    normed_all = gather_rows(normed)
    weight_in = jnp.concatenate(
        [
            query_weight.astype(jnp.bfloat16),
            key_value_matrix[0].astype(jnp.bfloat16),
            key_value_matrix[1].astype(jnp.bfloat16),
        ],
        axis=1,
    )
    projected = reduce_cols(jnp.dot(normed_all, weight_in, preferred_element_type=jnp.float32))
    query_rows = projected[:, :query_width].astype(jnp.bfloat16)
    keys_mine = projected[:, query_width : query_width + key_width].astype(jnp.bfloat16)
    values_mine = projected[:, query_width + key_width :].astype(jnp.bfloat16)
    keys_all, values_all = gather_cols((keys_mine, values_mine))
    col_index = lax.axis_index("col")
    positions = jnp.arange(rep_tokens, dtype=jnp.int32)
    query_pos = col_index * col_rows + jnp.arange(col_rows, dtype=jnp.int32)
    query_seq = lax.dynamic_slice_in_dim(seq_ids, col_index * col_rows, col_rows)
    allowed = (query_seq[:, None] == seq_ids[None, :]) & (positions[None, :] <= query_pos[:, None])

    def head_scores(head_index):
        head_query = query_rows[
            :, head_index * group_width * HEAD_SIZE : (head_index + 1) * group_width * HEAD_SIZE
        ].reshape(col_rows, group_width, HEAD_SIZE)
        head_keys = keys_all[:, head_index * HEAD_SIZE : (head_index + 1) * HEAD_SIZE]
        scores = (
            jnp.einsum("qgd,td->gqt", head_query, head_keys, preferred_element_type=jnp.float32)
            * scale_factor
        )
        return (head_query, head_keys, jnp.where(allowed[None], scores, masked_score))

    contexts = []
    totals = []
    for head_index in range(heads_here):
        head_query, head_keys, scores = head_scores(head_index)
        row_max = jnp.max(scores, axis=-1, keepdims=True)
        log_total = row_max + jnp.log(jnp.sum(jnp.exp(scores - row_max), axis=-1, keepdims=True))
        prob_low = jnp.exp(scores - log_total).astype(jnp.bfloat16)
        head_values = values_all[:, head_index * HEAD_SIZE : (head_index + 1) * HEAD_SIZE]
        contexts.append(
            jnp.einsum(
                "gqt,td->qgd", prob_low, head_values, preferred_element_type=jnp.float32
            ).reshape(col_rows, group_width * HEAD_SIZE)
        )
        totals.append(log_total)
    context = jnp.concatenate(contexts, axis=1).astype(jnp.bfloat16)
    context_all = gather_cols(context)
    out_low = out_weight.astype(jnp.bfloat16)
    attended = reduce_rows(jnp.dot(context_all, out_low, preferred_element_type=jnp.float32))
    middle = residual + attended
    second_scale = rms_scale(middle)
    normed_two = (middle * second_scale * norm_gains[1]).astype(jnp.bfloat16)
    normed_two_all = gather_rows(normed_two)
    slot_tokens, slot_weights = dispatch(routes, gate_probs, capacity, rep_tokens)
    padded = jnp.concatenate([normed_two_all, jnp.zeros((1, width_part), jnp.bfloat16)], axis=0)
    gate_up_all, down_all = (
        lax.all_gather(gate_up_weight.astype(jnp.bfloat16), "dp", axis=0, tiled=True),
        lax.all_gather(down_weight.astype(jnp.bfloat16), "dp", axis=0, tiled=True),
    )
    mixture = jnp.zeros((rep_tokens + 1, width_part), jnp.float32)
    kept_blocks = []
    for block_index in range(EXPERTS // expert_block):
        chosen = slice(block_index * expert_block, (block_index + 1) * expert_block)
        block_tokens = slot_tokens[:, chosen]
        block_weights = slot_weights[:, chosen]
        block_inputs = padded[block_tokens]
        block_gate_up = gate_up_all[chosen].reshape(expert_block, width_part, -1)
        block_down = down_all[chosen]

        def gate_terms(offset, piece_rows):
            return jnp.einsum(
                "ced,edf->cef", block_inputs, block_gate_up, preferred_element_type=jnp.float32
            )

        gate_up = reduce_slots(gate_terms, slot_rows)
        half_width = gate_up.shape[2] // 2
        hidden = (jax.nn.silu(gate_up[:, :, :half_width]) * gate_up[:, :, half_width:]).astype(
            jnp.bfloat16
        )

        def down_terms(running, shard_piece, offset):
            outputs = jnp.einsum(
                "cef,efd->ced", shard_piece, block_down, preferred_element_type=jnp.float32
            )
            weighted = (outputs * block_weights[:, :, None]).reshape(-1, width_part)
            return running + jax.ops.segment_sum(
                weighted, block_tokens.reshape(-1), num_segments=rep_tokens + 1
            )

        mixture = fold_slots(hidden, down_terms, mixture)
        kept_blocks.append((block_inputs, gate_up, hidden))
    expert_output = reduce_rows(mixture[:rep_tokens])
    block_output = (middle + expert_output).astype(jnp.bfloat16)
    grad_out_all = gather_rows(cotangent)
    grad_padded = jnp.concatenate([grad_out_all, jnp.zeros((1, width_part), jnp.bfloat16)], axis=0)
    gate_up_back, down_back = (
        lax.all_gather(gate_up_weight.astype(jnp.bfloat16), "dp", axis=0, tiled=True),
        lax.all_gather(down_weight.astype(jnp.bfloat16), "dp", axis=0, tiled=True),
    )
    token_grads = jnp.zeros((rep_tokens + 1, width_part), jnp.float32)
    gate_up_grads = []
    down_grads = []
    for block_index in range(EXPERTS // expert_block):
        chosen = slice(block_index * expert_block, (block_index + 1) * expert_block)
        block_tokens = slot_tokens[:, chosen]
        block_weights = slot_weights[:, chosen]
        block_gate_up = gate_up_back[chosen].reshape(expert_block, width_part, -1)
        block_down = down_back[chosen]
        block_inputs, gate_up, hidden = kept_blocks[block_index]
        half_width = gate_up.shape[2] // 2
        grad_slots = (
            grad_padded[block_tokens].astype(jnp.float32) * block_weights[:, :, None]
        ).astype(jnp.bfloat16)

        def hidden_terms(offset, piece_rows):
            return jnp.einsum(
                "ced,efd->cef", grad_slots, block_down, preferred_element_type=jnp.float32
            )

        grad_hidden = reduce_slots(hidden_terms, slot_rows)

        def down_weight_terms(running, shard_piece, offset):
            return jnp.einsum(
                "cef,ced->efd", shard_piece, grad_slots, preferred_element_type=jnp.float32
            )

        down_grads.append(
            fold_slots(
                hidden,
                down_weight_terms,
                jnp.zeros((expert_block, half_width, width_part), jnp.float32),
            )
        )
        gate_part = gate_up[:, :, :half_width]
        up_part = gate_up[:, :, half_width:]
        sigmoid_gate = jax.nn.sigmoid(gate_part)
        grad_gate = grad_hidden * up_part * sigmoid_gate * (1.0 + gate_part * (1.0 - sigmoid_gate))
        grad_up = grad_hidden * gate_part * sigmoid_gate
        grad_pair = jnp.concatenate([grad_gate, grad_up], axis=2).astype(jnp.bfloat16)

        def input_terms(running, shard_piece, offset):
            tokens_sum, weight_sum = running
            back_terms = jnp.einsum(
                "cef,edf->ced", shard_piece, block_gate_up, preferred_element_type=jnp.float32
            )
            tokens_sum = tokens_sum + jax.ops.segment_sum(
                back_terms.reshape(-1, width_part),
                block_tokens.reshape(-1),
                num_segments=rep_tokens + 1,
            )
            weight_sum = jnp.einsum(
                "ced,cef->edf", block_inputs, shard_piece, preferred_element_type=jnp.float32
            )
            return (tokens_sum, weight_sum)

        token_grads, weight_grad = fold_slots(
            grad_pair,
            input_terms,
            (token_grads, jnp.zeros((expert_block, width_part, 2 * half_width), jnp.float32)),
        )
        gate_up_grads.append(weight_grad)
    grad_gate_up_all = jnp.concatenate(gate_up_grads, axis=0).reshape(gate_up_all.shape)
    grad_down_all = jnp.concatenate(down_grads, axis=0)
    grad_gate_up, grad_down = (
        lax.psum_scatter(grad_gate_up_all, "dp", scatter_dimension=0, tiled=True),
        lax.psum_scatter(grad_down_all, "dp", scatter_dimension=0, tiled=True),
    )
    grad_normed_two = reduce_rows(token_grads[:rep_tokens])
    grad_middle_norm, grad_gain_two = norm_back(
        grad_normed_two, middle, second_scale, norm_gains[1]
    )
    grad_middle = cotangent.astype(jnp.float32) + grad_middle_norm
    grad_att_all = gather_rows(grad_middle.astype(jnp.bfloat16))
    grad_context = reduce_cols(
        jnp.einsum("td,hd->th", grad_att_all, out_low, preferred_element_type=jnp.float32)
    ).astype(jnp.bfloat16)
    grad_out = jnp.einsum(
        "th,td->hd", context_all, grad_att_all, preferred_element_type=jnp.float32
    )
    query_grads = []
    key_grads = []
    value_grads = []
    for head_index in range(heads_here):
        head_query, head_keys, scores = head_scores(head_index)
        prob_full = jnp.exp(scores - totals[head_index])
        prob_low = prob_full.astype(jnp.bfloat16)
        head_values = values_all[:, head_index * HEAD_SIZE : (head_index + 1) * HEAD_SIZE]
        head_grad = grad_context[
            :, head_index * group_width * HEAD_SIZE : (head_index + 1) * group_width * HEAD_SIZE
        ].reshape(col_rows, group_width, HEAD_SIZE)
        grad_prob = jnp.einsum(
            "qgd,td->gqt", head_grad, head_values, preferred_element_type=jnp.float32
        )
        inner = jnp.sum(prob_full * grad_prob, axis=-1, keepdims=True)
        grad_scores = (prob_full * (grad_prob - inner)).astype(jnp.bfloat16)
        query_grads.append(
            (
                jnp.einsum(
                    "gqt,td->qgd", grad_scores, head_keys, preferred_element_type=jnp.float32
                )
                * scale_factor
            ).reshape(col_rows, group_width * HEAD_SIZE)
        )
        key_grads.append(
            jnp.einsum("gqt,qgd->td", grad_scores, head_query, preferred_element_type=jnp.float32)
            * scale_factor
        )
        value_grads.append(
            jnp.einsum("gqt,qgd->td", prob_low, head_grad, preferred_element_type=jnp.float32)
        )
    key_grad, value_grad = reduce_cols(
        (jnp.concatenate(key_grads, axis=1), jnp.concatenate(value_grads, axis=1))
    )
    grad_in = jnp.concatenate(
        [jnp.concatenate(query_grads, axis=1), key_grad, value_grad], axis=1
    ).astype(jnp.bfloat16)
    grad_in_all = gather_cols(grad_in)
    grad_weight_in = jnp.einsum(
        "td,tf->df", normed_all, grad_in_all, preferred_element_type=jnp.float32
    )
    grad_normed = reduce_rows(
        jnp.einsum("tf,df->td", grad_in_all, weight_in, preferred_element_type=jnp.float32)
    )
    grad_input_norm, grad_gain_one = norm_back(grad_normed, residual, first_scale, norm_gains[0])
    input_grad = grad_middle + grad_input_norm
    gain_grad = lax.psum(jnp.stack([grad_gain_one, grad_gain_two]), ("dp", "row"))
    key_value_part = jnp.stack(
        [
            grad_weight_in[:, query_width : query_width + key_width],
            grad_weight_in[:, query_width + key_width :],
        ]
    )
    query_grad, key_value_grad, out_grad = lax.psum(
        (grad_weight_in[:, :query_width], key_value_part, grad_out), "dp"
    )
    matrix_rate = 1.5 * MODEL_WIDTH ** (-0.5)
    gains_moment_new, gains_second_new, gains_new = adam_update(
        norm_gains, gain_moment, gain_second, gain_grad, 0.5, 0.0
    )
    query_moment_new, query_second_new, query_new = adam_update(
        query_weight, query_moment, query_second, query_grad, matrix_rate, weight_decay
    )
    pair_moment_new, pair_second_new, pair_new = adam_update(
        key_value_matrix,
        key_value_first_moment,
        key_value_second_moment,
        key_value_grad,
        matrix_rate,
        weight_decay,
    )
    out_moment_new, out_second_new, out_new = adam_update(
        out_weight,
        out_moment,
        out_second,
        out_grad,
        1.5 * max(1, QUERY_HEADS * HEAD_SIZE // 256) ** (-0.5),
        weight_decay,
    )
    gate_moment_new, gate_second_new, gate_new = adam_update(
        gate_up_weight, gate_up_moment, gate_up_second, grad_gate_up, matrix_rate, weight_decay
    )
    down_moment_new, down_second_new, down_new = adam_update(
        down_weight, down_moment, down_second, grad_down, 1.5 * (FF // 16) ** (-0.5), weight_decay
    )
    return (
        block_output,
        input_grad,
        gains_moment_new,
        gains_second_new,
        gains_new,
        query_moment_new,
        query_second_new,
        query_new,
        pair_moment_new,
        pair_second_new,
        pair_new,
        out_moment_new,
        out_second_new,
        out_new,
        gate_moment_new,
        gate_second_new,
        gate_new,
        down_moment_new,
        down_second_new,
        down_new,
    )


def solution(mesh):
    return jax.shard_map(
        per_device,
        mesh=mesh,
        in_specs=(
            P(("dp", "row"), "col"),
            P(("dp", "row"), "col"),
            P("dp", None),
            P("dp", None),
            P("dp"),
            P(None, "col"),
            P(None, "col"),
            P(None, "col"),
            P("col", "row"),
            P("col", "row"),
            P("col", "row"),
            P(None, "col", "row"),
            P(None, "col", "row"),
            P(None, "col", "row"),
            P("row", "col"),
            P("row", "col"),
            P("row", "col"),
            P("dp", "col", None, "row"),
            P("dp", "col", None, "row"),
            P("dp", "col", None, "row"),
            P("dp", "row", "col"),
            P("dp", "row", "col"),
            P("dp", "row", "col"),
        ),
        out_specs=(
            P(("dp", "row"), "col"),
            P(("dp", "row"), "col"),
            P(None, "col"),
            P(None, "col"),
            P(None, "col"),
            P("col", "row"),
            P("col", "row"),
            P("col", "row"),
            P(None, "col", "row"),
            P(None, "col", "row"),
            P(None, "col", "row"),
            P("row", "col"),
            P("row", "col"),
            P("row", "col"),
            P("dp", "col", None, "row"),
            P("dp", "col", None, "row"),
            P("dp", "col", None, "row"),
            P("dp", "row", "col"),
            P("dp", "row", "col"),
            P("dp", "row", "col"),
        ),
        check_vma=False,
    )
```

profile of v0, /device:TPU:0, one launch (start us, length us, event | category | flops | bytes accessed | tf_op | source)
XLA Modules:
  0.0 2514.7 jit_solution(1561073917929574109)
XLA Ops:
  42.1 107.9 %reduce-scatter.19.cloned.1.call-done = f32[384,1024]{1,0:T(8,128)} async-done(((f32[1536,1024]{1,0:T(8,128)}), f32[384,1024]{1,0:T(8,128)}) %reduce-scatter.19.cloned.1.call-update) | async-done | bytes 1572880 | tf_op jit(solution)/shard_map/reduce_scatter | solution.py:62
  206.1 33.3 %all-gather.13.cloned.1.call-done = bf16[1536,512]{0,1:T(8,128)(2,1)} async-done(((bf16[384,512]{0,1:T(8,128)(2,1)}), bf16[1536,512]{0,1:T(8,128)(2,1)}) %all-gather.13.cloned.1.call-update) | async-done | bytes 1572880 | tf_op jit(solution)/shard_map/all_gather | solution.py:56
  252.4 84.9 %gather_fusion = s32[15360]{0:T(1024)S(1)} fusion(s32[12288]{0:T(1024)S(1)} %get-tuple-element.21, s32[15360]{0:T(1024)S(1)} %broadcast_clamp_fusion.1), kind=kCustom, calls=%fused_computation | custom fusion | bytes 184320 | tf_op jit(solution)/shard_map/gather | solution.py:87
  448.7 71.5 %reduce-scatter.23.cloned.1.call-done = f32[120,8,512]{2,0,1:T(8,128)} async-done(((f32[480,8,512]{2,0,1:T(8,128)}), f32[120,8,512]{2,0,1:T(8,128)}) %reduce-scatter.23.cloned.1.call-update) | async-done | bytes 1966096 | tf_op jit(solution)/shard_map/reduce_scatter | solution.py:66
  522.9 136.4 %reduce-scatter.25.cloned.1.call-done = f32[120,8,512]{2,0,1:T(8,128)} async-done(((f32[480,8,512]{2,0,1:T(8,128)}), f32[120,8,512]{2,0,1:T(8,128)}) %reduce-scatter.25.cloned.1.call-update) | async-done | bytes 1966096 | tf_op jit(solution)/shard_map/reduce_scatter | solution.py:66
  662.0 136.6 %reduce-scatter.27.cloned.1.call-done = f32[120,8,512]{2,0,1:T(8,128)} async-done(((f32[480,8,512]{2,0,1:T(8,128)}), f32[120,8,512]{2,0,1:T(8,128)}) %reduce-scatter.27.cloned.1.call-update) | async-done | bytes 1966096 | tf_op jit(solution)/shard_map/reduce_scatter | solution.py:66
  860.5 84.9 %gather_fusion.2 = f32[15360]{0:T(1024)S(1)} fusion(f32[12288]{0:T(1024)S(1)} %reshape.350, s32[15360]{0:T(1024)S(1)} %broadcast_clamp_fusion), kind=kCustom, calls=%fused_computation.2 | custom fusion | bytes 184320 | tf_op jit(solution)/shard_map/gather | solution.py:90
  988.6 39.9 %all-gather.21.cloned.1.call-done = bf16[480,8,256]{2,0,1:T(8,128)(2,1)} async-done(((bf16[120,8,256]{2,0,1:T(8,128)(2,1)}), bf16[480,8,256]{2,0,1:T(8,128)(2,1)}) %all-gather.21.cloned.1.call-update) | async-done | bytes 1966096 | tf_op jit(solution)/shard_map/all_gather | solution.py:75
  1034.4 38.7 %all-gather.23.cloned.1.call-done = bf16[480,8,256]{2,0,1:T(8,128)(2,1)} async-done(((bf16[120,8,256]{2,0,1:T(8,128)(2,1)}), bf16[480,8,256]{2,0,1:T(8,128)(2,1)}) %all-gather.23.cloned.1.call-update) | async-done | bytes 1966096 | tf_op jit(solution)/shard_map/all_gather | solution.py:75
  1079.1 38.6 %all-gather.25.cloned.1.call-done = bf16[480,8,256]{2,0,1:T(8,128)(2,1)} async-done(((bf16[120,8,256]{2,0,1:T(8,128)(2,1)}), bf16[480,8,256]{2,0,1:T(8,128)(2,1)}) %all-gather.25.cloned.1.call-update) | async-done | bytes 1966096 | tf_op jit(solution)/shard_map/all_gather | solution.py:75
  1126.4 70.7 %reduce-scatter.53.cloned.1.call-done = f32[8,256,256]{2,1,0:T(8,128)} async-done(((f32[32,256,256]{2,1,0:T(8,128)}), f32[8,256,256]{2,1,0:T(8,128)}) %reduce-scatter.53.cloned.1.call-update) | async-done | bytes 2097168 | tf_op jit(solution)/shard_map/reduce_scatter | solution.py:307
  1204.2 34.4 %all-gather.19.cloned.1.call-done = bf16[32,256,256]{2,1,0:T(8,128)(2,1)} async-done(((bf16[8,256,256]{2,1,0:T(8,128)(2,1)}), bf16[32,256,256]{2,1,0:T(8,128)(2,1)}) %all-gather.19.cloned.1.call-update) | async-done | bytes 4194320 | tf_op jit(solution)/shard_map/all_gather | solution.py:199
  1262.3 54.9 %reduce-scatter.33.cloned.1.call-done = f32[120,8,256]{2,0,1:T(8,128)} async-done(((f32[480,8,256]{2,0,1:T(8,128)}), f32[120,8,256]{2,0,1:T(8,128)}) %reduce-scatter.33.cloned.1.call-update) | async-done | bytes 983056 | tf_op jit(solution)/shard_map/reduce_scatter | solution.py:66
  1320.5 71.9 %reduce-scatter.35.cloned.1.call-done = f32[120,8,256]{2,0,1:T(8,128)} async-done(((f32[480,8,256]{2,0,1:T(8,128)}), f32[120,8,256]{2,0,1:T(8,128)}) %reduce-scatter.35.cloned.1.call-update) | async-done | bytes 983056 | tf_op jit(solution)/shard_map/reduce_scatter | solution.py:66
  1395.2 73.0 %reduce-scatter.39.cloned.1.call-done = f32[120,8,256]{2,0,1:T(8,128)} async-done(((f32[480,8,256]{2,0,1:T(8,128)}), f32[120,8,256]{2,0,1:T(8,128)}) %reduce-scatter.39.cloned.1.call-update) | async-done | bytes 983056 | tf_op jit(solution)/shard_map/reduce_scatter | solution.py:66
  1471.0 73.0 %reduce-scatter.37.cloned.1.call-done = f32[120,8,256]{2,0,1:T(8,128)} async-done(((f32[480,8,256]{2,0,1:T(8,128)}), f32[120,8,256]{2,0,1:T(8,128)}) %reduce-scatter.37.cloned.1.call-update) | async-done | bytes 983056 | tf_op jit(solution)/shard_map/reduce_scatter | solution.py:66
  1548.8 74.1 %all-gather.27.cloned.1.call-done = bf16[480,8,512]{2,0,1:T(8,128)(2,1)} async-done(((bf16[120,8,512]{2,0,1:T(8,128)(2,1)}), bf16[480,8,512]{2,0,1:T(8,128)(2,1)}) %all-gather.27.cloned.1.call-update) | async-done | bytes 3932176 | tf_op jit(solution)/shard_map/all_gather | solution.py:75
  1654.8 44.6 %all-gather.29.cloned.1.call-done = bf16[480,8,512]{2,0,1:T(8,128)(2,1)} async-done(((bf16[120,8,512]{2,0,1:T(8,128)(2,1)}), bf16[480,8,512]{2,0,1:T(8,128)(2,1)}) %all-gather.29.cloned.1.call-update) | async-done | bytes 3932176 | tf_op jit(solution)/shard_map/all_gather | solution.py:75
  1735.2 40.8 %all-gather.33.cloned.1.call-done = bf16[480,8,512]{2,0,1:T(8,128)(2,1)} async-done(((bf16[120,8,512]{2,0,1:T(8,128)(2,1)}), bf16[480,8,512]{2,0,1:T(8,128)(2,1)}) %all-gather.33.cloned.1.call-update) | async-done | bytes 3932176 | tf_op jit(solution)/shard_map/all_gather | solution.py:75
  1808.0 44.7 %all-gather.31.cloned.1.call-done = bf16[480,8,512]{2,0,1:T(8,128)(2,1)} async-done(((bf16[120,8,512]{2,0,1:T(8,128)(2,1)}), bf16[480,8,512]{2,0,1:T(8,128)(2,1)}) %all-gather.31.cloned.1.call-update) | async-done | bytes 3932176 | tf_op jit(solution)/shard_map/all_gather | solution.py:75
  2062.0 60.1 %reduce-scatter.43.cloned.1.call-done = f32[384,512]{1,0:T(8,128)} async-done(((f32[1536,512]{1,0:T(8,128)}), f32[384,512]{1,0:T(8,128)}) %reduce-scatter.43.cloned.1.call-update) | async-done | bytes 786448 | tf_op jit(solution)/shard_map/reduce_scatter | solution.py:62
  2180.3 34.8 %reduce-scatter.47.cloned.1.call-done = f32[384,256]{0,1:T(8,128)} async-done(((f32[1536,256]{0,1:T(8,128)}), f32[384,256]{0,1:T(8,128)}) %reduce-scatter.47.cloned.1.call-update) | async-done | bytes 393232 | tf_op jit(solution)/shard_map/reduce_scatter | solution.py:62
  2219.9 59.7 %all-gather.35.cloned.1.call-done = bf16[1536,1024]{0,1:T(8,128)(2,1)} async-done(((bf16[384,1024]{0,1:T(8,128)(2,1)}), bf16[1536,1024]{0,1:T(8,128)(2,1)}) %all-gather.35.cloned.1.call-update) | async-done | bytes 3145744 | tf_op jit(solution)/shard_map/all_gather | solution.py:56
  2384.2 99.8 %reduce-scatter.51.cloned.1.call-done = f32[8,256,2,256]{3,1,2,0:T(8,128)} async-done(((f32[32,256,2,256]{3,1,2,0:T(8,128)}), f32[8,256,2,256]{3,1,2,0:T(8,128)}) %reduce-scatter.51.cloned.1.call-update) | async-done | bytes 4194320 | tf_op jit(solution)/shard_map/reduce_scatter | solution.py:306
  (548 shorter events, 889.0 us)
Async XLA Ops:
  7.2 142.8 %reduce-scatter.19.cloned.1.call-start = ((), (), s32[]{:S(2)}) async-start(), calls=%async_computation.18 | async-start | bytes 7864320 | tf_op jit(solution)/shard_map/reduce_scatter | solution.py:62
  40.8 198.6 %all-gather.13.cloned.1.call-start = ((), (), s32[]{:S(2)}) async-start(), calls=%async_computation.19 | async-start | bytes 1966080 | tf_op jit(solution)/shard_map/all_gather | solution.py:56
  202.1 137.0 %all-gather.15.cloned.1.call-start = ((), (), s32[]{:S(2)}) async-start(), calls=%async_computation.21 | async-start | bytes 10485760 | tf_op jit(solution)/shard_map/all_gather | solution.py:198
  206.1 140.2 %reduce-scatter.21.cloned.1.call-start = ((), (), s32[]{:S(2)}) async-start(), calls=%async_computation.20 | async-start | bytes 2359296 | tf_op jit(solution)/shard_map/reduce_scatter | solution.py:50
  242.6 277.7 %reduce-scatter.23.cloned.1.call-start = ((), (), s32[]{:S(2)}) async-start(), calls=%async_computation.22 | async-start | bytes 9830400 | tf_op jit(solution)/shard_map/reduce_scatter | solution.py:66
  385.6 273.7 %reduce-scatter.25.cloned.1.call-start = ((), (), s32[]{:S(2)}) async-start(), calls=%async_computation.25 | async-start | bytes 9830400 | tf_op jit(solution)/shard_map/reduce_scatter | solution.py:66
  406.6 391.9 %reduce-scatter.27.cloned.1.call-start = ((), (), s32[]{:S(2)}) async-start(), calls=%async_computation.27 | async-start | bytes 9830400 | tf_op jit(solution)/shard_map/reduce_scatter | solution.py:66
  427.7 517.8 %reduce-scatter.29.cloned.1.call-start = ((), (), s32[]{:S(2)}) async-start(), calls=%async_computation.29 | async-start | bytes 9830400 | tf_op jit(solution)/shard_map/reduce_scatter | solution.py:66
  448.7 535.4 %all-gather.17.cloned.1.call-start = ((), (), s32[]{:S(2)}) async-start(), calls=%async_computation.23 | async-start | bytes 2457600 | tf_op jit(solution)/shard_map/all_gather | solution.py:75
  522.8 505.7 %all-gather.21.cloned.1.call-start = ((), (), s32[]{:S(2)}) async-start(), calls=%async_computation.26 | async-start | bytes 2457600 | tf_op jit(solution)/shard_map/all_gather | solution.py:75
  661.9 411.3 %all-gather.23.cloned.1.call-start = ((), (), s32[]{:S(2)}) async-start(), calls=%async_computation.28 | async-start | bytes 2457600 | tf_op jit(solution)/shard_map/all_gather | solution.py:75
  801.1 316.6 %all-gather.25.cloned.1.call-start = ((), (), s32[]{:S(2)}) async-start(), calls=%async_computation.30 | async-start | bytes 2457600 | tf_op jit(solution)/shard_map/all_gather | solution.py:75
  948.2 248.8 %reduce-scatter.53.cloned.1.call-start = ((), (), s32[]{:S(2)}) async-start(), calls=%async_computation.47 | async-start | bytes 10485760 | tf_op jit(solution)/shard_map/reduce_scatter | solution.py:307
  1244.4 148.0 %reduce-scatter.35.cloned.1.call-start = ((), (), s32[]{:S(2)}) async-start(), calls=%async_computation.34 | async-start | bytes 4915200 | tf_op jit(solution)/shard_map/reduce_scatter | solution.py:66
  1250.2 218.0 %reduce-scatter.39.cloned.1.call-start = ((), (), s32[]{:S(2)}) async-start(), calls=%async_computation.38 | async-start | bytes 4915200 | tf_op jit(solution)/shard_map/reduce_scatter | solution.py:66
  1256.4 287.6 %reduce-scatter.37.cloned.1.call-start = ((), (), s32[]{:S(2)}) async-start(), calls=%async_computation.36 | async-start | bytes 4915200 | tf_op jit(solution)/shard_map/reduce_scatter | solution.py:66
  1262.2 360.7 %all-gather.27.cloned.1.call-start = ((), (), s32[]{:S(2)}) async-start(), calls=%async_computation.33 | async-start | bytes 4915200 | tf_op jit(solution)/shard_map/all_gather | solution.py:75
  1320.5 378.9 %all-gather.29.cloned.1.call-start = ((), (), s32[]{:S(2)}) async-start(), calls=%async_computation.35 | async-start | bytes 4915200 | tf_op jit(solution)/shard_map/all_gather | solution.py:75
  1395.1 380.9 %all-gather.33.cloned.1.call-start = ((), (), s32[]{:S(2)}) async-start(), calls=%async_computation.39 | async-start | bytes 4915200 | tf_op jit(solution)/shard_map/all_gather | solution.py:75
  1471.0 381.7 %all-gather.31.cloned.1.call-start = ((), (), s32[]{:S(2)}) async-start(), calls=%async_computation.37 | async-start | bytes 4915200 | tf_op jit(solution)/shard_map/all_gather | solution.py:75
  1547.3 472.5 %reduce-scatter.41.cloned.1.call-start = ((), (), s32[]{:S(2)}) async-start(), calls=%async_computation.40 | async-start | bytes 2359296 | tf_op jit(solution)/shard_map/reduce_scatter | solution.py:50
  1889.7 154.6 %reduce-scatter.31.cloned.1.call-start = ((), (), s32[]{:S(2)}) async-start(), calls=%async_computation.31 | async-start | bytes 2359296 | tf_op jit(solution)/shard_map/reduce_scatter | solution.py:50
  2155.7 123.9 %all-gather.35.cloned.1.call-start = ((), (), s32[]{:S(2)}) async-start(), calls=%async_computation.44 | async-start | bytes 3932160 | tf_op jit(solution)/shard_map/all_gather | solution.py:56
  2288.6 195.5 %reduce-scatter.51.cloned.1.call-start = ((), (), s32[]{:S(2)}) async-start(), calls=%async_computation.46 | async-start | bytes 20971520 | tf_op jit(solution)/shard_map/reduce_scatter | solution.py:306
  (136 other events, 5862.3 us)
Sparse Core Ops, SparseCore 0:
  40.9 108.9 reduce-scatter.18
  202.2 37.1 all-gather.12
  241.5 57.5 all-gather.14
  385.7 134.4 reduce-scatter.22
  522.5 136.7 reduce-scatter.24
  661.7 136.7 reduce-scatter.26
  800.9 136.7 reduce-scatter.28
  939.9 44.0 all-gather.16
  986.1 42.3 all-gather.20
  1030.8 42.3 all-gather.22
  1075.3 42.3 all-gather.24
  1126.5 70.5 reduce-scatter.52
  1244.5 72.6 reduce-scatter.32
  1319.3 73.0 reduce-scatter.34
  1395.1 73.0 reduce-scatter.38
  1470.9 73.0 reduce-scatter.36
  1546.1 76.7 all-gather.26
  1624.4 74.9 all-gather.28
  1701.0 75.0 all-gather.32
  1777.6 74.9 all-gather.30
  2061.9 60.2 reduce-scatter.42
  2217.3 62.2 all-gather.34
  2284.4 41.8 all-reduce.4
  2357.9 126.1 reduce-scatter.50
  (7 shorter events, 205.0 us)
where the time goes:
time: 2520 us; the launch traced here: 2510 us
  waiting for transfers between devices  1520 us (60%)
  other arithmetic  337 us (13%)
  local copies, waits for them, and re-layouts  324 us (13%)
  matrix products  173 us (7%)
  blocking collectives  136 us (5%)
    reduce_scatter x8, waiting for transfers between devices, reduce_slots(): lax.psum_scatter(term_fn(jnp.int32(0), slot_rows * lax.axis_size('col')),...  617 us
    all_gather x8, waiting for transfers between devices, fold_slots(): lax.all_gather(value_rows, 'col', axis=0, tiled=True)  345 us
    reduce_scatter x4, waiting for transfers between devices, reduce_cols(): return lax.psum_scatter(value_rows, 'col', scatter_dimension=0, tiled=True)  216 us
    scatter-add x4, other arithmetic, input_terms(): jax.ops.segment_sum(back_terms.reshape(-1, width_part), block_tokens.resh...  109 us
    scatter-add x4, other arithmetic, down_terms(): jax.ops.segment_sum(weighted, block_tokens.reshape(-1), num_segments=rep_...  108 us
    reduce_scatter x1, waiting for transfers between devices, per_device(): lax.psum_scatter(grad_gate_up_all, 'dp', scatter_dimension=0, tiled=True)  99.8 us
    all_gather x2, waiting for transfers between devices, gather_cols(): lax.all_gather(shortened(value_rows), 'col', axis=0, tiled=True)  93 us
    gather x3, local copies, waits for them, and re-layouts, dispatch(): source = sorted_order[position]  85.1 us
  transfers between devices with their start and end apart: 31, of which 27 were waited for; matrix products, arithmetic and copies ran while one was open for 27% of the time, Pallas kernels for 0%

commit v1 on v0

v1 whole, which is shorter than its diff:
```python
import jax
import jax.numpy as jnp
from jax import lax
from jax.sharding import PartitionSpec as P

MODEL_WIDTH = 1024
QUERY_HEADS = 16
KEY_VALUE_HEADS = 8
HEAD_SIZE = 64
FF = 512
EXPERTS = 32
TOP = 8
STEP = 10


norm_epsilon = 1e-06
first_decay = 0.9
second_decay = 0.95
adam_epsilon = 1e-08
weight_decay = 0.1
masked_score = -1e30
grid_axes = ("row", "col")
query_block = 384


def low(value):
    return value.astype(jnp.bfloat16)


def product(formula, left, right):
    return jnp.einsum(formula, left, right, preferred_element_type=jnp.float32)


def grid_split(rows):
    row_count, col_count = lax.axis_size("row"), lax.axis_size("col")
    tokens, width = rows.shape
    blocks = rows.reshape(row_count, tokens // row_count, col_count, width // col_count)
    return blocks.transpose(0, 2, 1, 3).reshape(
        row_count * col_count, tokens // row_count, width // col_count
    )


def grid_whole(block):
    row_count, col_count = lax.axis_size("row"), lax.axis_size("col")
    tokens, width = block.shape
    blocks = lax.all_gather(block, grid_axes, axis=0, tiled=False)
    blocks = blocks.reshape(row_count, col_count, tokens, width).transpose(0, 2, 1, 3)
    return blocks.reshape(row_count * tokens, col_count * width)


def grid_exchange(blocks):
    return lax.all_to_all(blocks, grid_axes, split_axis=0, concat_axis=0, tiled=True)


def col_exchange(blocks):
    return lax.all_to_all(blocks, "col", split_axis=0, concat_axis=0, tiled=True)


def grid_total(blocks):
    return lax.psum_scatter(blocks, grid_axes, scatter_dimension=0, tiled=True)


def own_rows(value_rows, index, count):
    return lax.dynamic_slice_in_dim(value_rows, index * count, count, axis=0)


def whole_experts(blocks):
    grid = lax.axis_size("row") * lax.axis_size("col")
    if blocks.shape[0] % grid == 0:
        split = blocks.reshape(-1, grid, *blocks.shape[1:]).swapaxes(0, 1)
        return grid_exchange(split).swapaxes(0, 1), True
    every = lax.all_gather(blocks, "dp", axis=0, tiled=True)
    split = every.reshape(-1, grid, *every.shape[1:]).swapaxes(0, 1)
    return grid_exchange(split).swapaxes(0, 1), False


def expert_blocks(grads, experts_here):
    grid = grads.shape[1]
    if experts_here % grid == 0:
        mine = lax.psum_scatter(grads, "dp", scatter_dimension=0, tiled=True)
        mine = grid_exchange(mine.swapaxes(0, 1)).swapaxes(0, 1)
        return mine.reshape(experts_here, *grads.shape[2:])
    every = grid_exchange(grads.swapaxes(0, 1)).swapaxes(0, 1)
    every = every.reshape(-1, *grads.shape[2:])
    return lax.psum_scatter(every, "dp", scatter_dimension=0, tiled=True)


def attend(query_rows, key_rows, value_rows, allowed_blocks, scale_factor):
    contexts, totals = [], []
    tokens = key_rows.shape[0]
    for start in range(0, tokens, query_block):
        stop = start + query_block
        scores = product("gqd,td->gqt", query_rows[:, start:stop], key_rows[:stop]) * scale_factor
        scores = jnp.where(allowed_blocks[start // query_block], scores, masked_score)
        row_max = jnp.max(scores, axis=-1, keepdims=True)
        log_total = row_max + jnp.log(jnp.sum(jnp.exp(scores - row_max), axis=-1, keepdims=True))
        prob_low = low(jnp.exp(scores - log_total))
        contexts.append(low(product("gqt,td->gqd", prob_low, value_rows[:stop])))
        totals.append(log_total)
    return jnp.concatenate(contexts, axis=1), totals


def attend_back(query_rows, key_rows, value_rows, grad_rows, totals, allowed_blocks, scale_factor):
    tokens = key_rows.shape[0]
    grad_queries = []
    grad_keys = jnp.zeros(key_rows.shape, jnp.float32)
    grad_values = jnp.zeros(key_rows.shape, jnp.float32)
    for start in range(0, tokens, query_block):
        stop = start + query_block
        block_query = query_rows[:, start:stop]
        block_grad = grad_rows[:, start:stop]
        scores = product("gqd,td->gqt", block_query, key_rows[:stop]) * scale_factor
        scores = jnp.where(allowed_blocks[start // query_block], scores, masked_score)
        full = jnp.exp(scores - totals[start // query_block])
        grad_prob = product("gqd,td->gqt", block_grad, value_rows[:stop])
        inner = jnp.sum(full * grad_prob, axis=-1, keepdims=True)
        grad_scores = low(full * (grad_prob - inner))
        grad_queries.append(product("gqt,td->gqd", grad_scores, key_rows[:stop]) * scale_factor)
        rest = ((0, tokens - stop), (0, 0))
        grad_keys = grad_keys + jnp.pad(product("gqt,gqd->td", grad_scores, block_query), rest)
        grad_values = grad_values + jnp.pad(product("gqt,gqd->td", low(full), block_grad), rest)
    return jnp.concatenate(grad_queries, axis=1), grad_keys * scale_factor, grad_values


def adam_update(weight, moment, second, gradient, step_rate, decay_rate):
    moment_new = first_decay * moment + (1.0 - first_decay) * gradient
    second_new = second_decay * second + (1.0 - second_decay) * gradient * gradient
    step_size = step_rate / (1.0 - first_decay**STEP)
    denominator = jnp.sqrt(second_new / (1.0 - second_decay**STEP)) + adam_epsilon
    weight_new = weight - step_size * moment_new / denominator - step_rate * decay_rate * weight
    return (moment_new, second_new, weight_new)


def per_device(
    inputs,
    cotangent,
    routes,
    gate_probs,
    seq_ids,
    norm_gains,
    gain_moment,
    gain_second,
    query_weight,
    query_moment,
    query_second,
    key_value_matrix,
    key_value_first_moment,
    key_value_second_moment,
    out_weight,
    out_moment,
    out_second,
    gate_up_weight,
    gate_up_moment,
    gate_up_second,
    down_weight,
    down_moment,
    down_second,
):
    rep_tokens = routes.shape[0]
    row_count, col_count = lax.axis_size("row"), lax.axis_size("col")
    grid = row_count * col_count
    row_index, col_index = lax.axis_index("row"), lax.axis_index("col")
    place = row_index * col_count + col_index
    width_part = inputs.shape[1]
    key_width = key_value_matrix.shape[2]
    group_width = QUERY_HEADS // KEY_VALUE_HEADS
    head_span = group_width * HEAD_SIZE
    scale_factor = HEAD_SIZE ** (-0.5)
    capacity = rep_tokens * TOP // EXPERTS * 5 // 4
    own_count = EXPERTS // grid
    part_tokens = rep_tokens // grid
    half_tokens = rep_tokens // row_count
    ff_part = down_weight.shape[1]
    experts_here = gate_up_weight.shape[0]
    heads_here = key_width // HEAD_SIZE
    weight_in_here = low(
        jnp.concatenate(
            [
                query_weight.reshape(width_part, heads_here, head_span),
                key_value_matrix[0].reshape(width_part, heads_here, HEAD_SIZE),
                key_value_matrix[1].reshape(width_part, heads_here, HEAD_SIZE),
            ],
            axis=2,
        )
    ).transpose(1, 0, 2)
    head_width = weight_in_here.shape[2]
    inputs_all = grid_whole(inputs)
    weight_in_all = lax.all_gather(weight_in_here, grid_axes, axis=0, tiled=False)
    weight_in_all = (
        weight_in_all.reshape(row_count, col_count, heads_here, width_part, head_width)
        .transpose(0, 2, 1, 3, 4)
        .reshape(grid, MODEL_WIDTH, head_width)
    )
    weight_in = lax.dynamic_index_in_dim(weight_in_all, place, axis=0, keepdims=False)
    out_all = grid_whole(low(out_weight))
    expert_weights = low(
        jnp.concatenate(
            [gate_up_weight.reshape(experts_here, width_part, 2 * ff_part), down_weight], axis=2
        )
    )
    expert_weights, spread = whole_experts(expert_weights)
    gate_up_mine = (
        expert_weights[..., : 2 * ff_part]
        .reshape(-1, row_count, col_count * width_part, 2, ff_part)
        .transpose(0, 2, 3, 1, 4)
        .reshape(-1, MODEL_WIDTH, 2 * FF)
    )
    down_mine = (
        expert_weights[..., 2 * ff_part :]
        .reshape(-1, row_count, col_count, ff_part, width_part)
        .transpose(0, 1, 3, 2, 4)
        .reshape(-1, FF, MODEL_WIDTH)
    )
    if spread:
        gate_up_mine = lax.all_gather(gate_up_mine, "dp", axis=0, tiled=True)
        down_mine = lax.all_gather(down_mine, "dp", axis=0, tiled=True)
    cotangent_all = grid_whole(cotangent)
    gains_all = lax.all_gather(norm_gains, "col", axis=1, tiled=True)

    own_ids = jnp.arange(own_count, dtype=jnp.int32) * grid + place
    named = routes[:, :, None] == own_ids[None, None, :]
    token_weights = jnp.sum(jnp.where(named, gate_probs[:, :, None], 0.0), axis=1)
    chosen = jnp.any(named, axis=1)
    positions = jnp.arange(rep_tokens, dtype=jnp.int32)
    earlier = low(positions[:, None] > positions[None, :])
    slot_of = product("ts,si->it", earlier, low(chosen)).astype(jnp.int32)
    slot_of = jnp.where(chosen.T, slot_of, -1)
    slots = jnp.arange(capacity, dtype=jnp.int32)
    filled = slot_of[:, None, :] == slots[None, :, None]
    slot_weights = jnp.sum(jnp.where(filled, token_weights.T[:, None, :], 0.0), axis=2)[..., None]
    pick = low(filled)

    residual = inputs_all.astype(jnp.float32)
    first_scale = lax.rsqrt(jnp.mean(residual * residual, axis=1, keepdims=True) + norm_epsilon)
    normed = low(residual * first_scale * gains_all[0])
    projected = low(product("td,df->tf", normed, weight_in))
    query_rows = projected[:, :head_span].reshape(rep_tokens, group_width, HEAD_SIZE)
    query_rows = query_rows.transpose(1, 0, 2)
    key_rows = projected[:, head_span : head_span + HEAD_SIZE]
    value_rows = projected[:, head_span + HEAD_SIZE :]
    allowed_blocks = [
        (seq_ids[start : start + query_block, None] == seq_ids[None, : start + query_block])
        & (
            positions[None, : start + query_block]
            <= positions[start : start + query_block, None]
        )
        for start in range(0, rep_tokens, query_block)
    ]
    context, totals = attend(query_rows, key_rows, value_rows, allowed_blocks, scale_factor)
    context = context.transpose(1, 0, 2).reshape(rep_tokens, head_span)
    context_all = lax.all_gather(context, grid_axes, axis=1, tiled=True)
    middle = residual + product("th,hd->td", context_all, out_all)
    second_scale = lax.rsqrt(jnp.mean(middle * middle, axis=1, keepdims=True) + norm_epsilon)
    normed_two = low(middle * second_scale * gains_all[1])

    slot_inputs = low(product("ist,td->isd", pick, normed_two))
    gate_up = product("isd,idf->isf", slot_inputs, gate_up_mine)
    gate_part, up_part = gate_up[..., :FF], gate_up[..., FF:]
    hidden = low(jax.nn.silu(gate_part) * up_part)
    expert_out = low(product("isf,ifd->isd", hidden, down_mine) * slot_weights)
    mixture = low(product("ist,isd->td", pick, expert_out))
    mixture = grid_total(grid_split(mixture).reshape(-1, width_part))
    middle_here = lax.dynamic_slice(
        middle, (row_index * half_tokens, col_index * width_part), (half_tokens, width_part)
    )
    block_output = low(middle_here + mixture.astype(jnp.float32))

    grad_slots = low(product("ist,td->isd", pick, cotangent_all) * slot_weights)
    grad_hidden = product("isd,ifd->isf", grad_slots, down_mine)
    sigmoid_gate = jax.nn.sigmoid(gate_part)
    grad_gate = grad_hidden * up_part * sigmoid_gate * (1.0 + gate_part * (1.0 - sigmoid_gate))
    grad_up = grad_hidden * gate_part * sigmoid_gate
    grad_pair = low(jnp.concatenate([grad_gate, grad_up], axis=2))
    back_slots = low(product("isf,idf->isd", grad_pair, gate_up_mine))
    grad_normed_two = low(product("ist,isd->td", pick, back_slots))
    grad_normed_two = grid_total(grad_normed_two).astype(jnp.float32)
    down_grads = low(product("isf,isd->ifd", hidden, grad_slots))
    gate_up_grads = low(product("isd,isf->idf", slot_inputs, grad_pair))
    gate_up_grads = gate_up_grads.reshape(
        own_count, col_count, width_part, 2, row_count, ff_part
    ).transpose(0, 4, 1, 2, 3, 5)
    gate_up_grads = gate_up_grads.reshape(own_count, grid, width_part, 2 * ff_part)
    down_grads = down_grads.reshape(
        own_count, row_count, ff_part, col_count, width_part
    ).transpose(0, 1, 3, 2, 4)
    down_grads = down_grads.reshape(own_count, grid, ff_part, width_part)
    grad_gate_up = expert_blocks(gate_up_grads, experts_here).astype(jnp.float32)
    grad_gate_up = grad_gate_up.reshape(gate_up_weight.shape)
    grad_down = expert_blocks(down_grads, experts_here).astype(jnp.float32)

    middle_part = own_rows(middle, place, part_tokens)
    scale_part = own_rows(second_scale, place, part_tokens)
    inner = jnp.sum(grad_normed_two * gains_all[1] * middle_part, axis=1, keepdims=True)
    grad_middle = (
        own_rows(cotangent_all, place, part_tokens).astype(jnp.float32)
        + scale_part * gains_all[1] * grad_normed_two
        - middle_part * scale_part**3 * inner / MODEL_WIDTH
    )
    grad_gain_two = jnp.sum(grad_normed_two * middle_part * scale_part, axis=0)
    grad_middle_all = lax.all_gather(low(grad_middle), grid_axes, axis=0, tiled=True)

    out_mine = own_rows(out_all, place, head_span)
    grad_context = low(product("td,hd->th", grad_middle_all, out_mine))
    out_grads = product("th,td->hd", context, grad_middle_all)
    grad_context = grad_context.reshape(rep_tokens, group_width, HEAD_SIZE).transpose(1, 0, 2)
    grad_queries, grad_keys, grad_values = attend_back(
        query_rows, key_rows, value_rows, grad_context, totals, allowed_blocks, scale_factor
    )
    grad_queries = grad_queries.transpose(1, 0, 2).reshape(rep_tokens, head_span)
    grad_in = low(jnp.concatenate([grad_queries, grad_keys, grad_values], axis=1))
    grad_in_part = grid_exchange(grad_in.reshape(grid, part_tokens, head_width))
    weight_in_grads = product("td,tf->df", normed, grad_in)
    grad_normed = product("htf,hdf->td", grad_in_part, weight_in_all)

    residual_part = own_rows(residual, place, part_tokens)
    scale_part = own_rows(first_scale, place, part_tokens)
    inner = jnp.sum(grad_normed * gains_all[0] * residual_part, axis=1, keepdims=True)
    input_grad = (
        grad_middle
        + scale_part * gains_all[0] * grad_normed
        - residual_part * scale_part**3 * inner / MODEL_WIDTH
    )
    grad_gain_one = jnp.sum(grad_normed * residual_part * scale_part, axis=0)
    input_grad = input_grad.reshape(part_tokens, col_count, width_part).transpose(1, 0, 2)
    input_grad = col_exchange(input_grad).reshape(half_tokens, width_part)
    gain_grad = lax.psum(jnp.stack([grad_gain_one, grad_gain_two]), ("dp", "row", "col"))
    gain_grad = lax.dynamic_slice_in_dim(gain_grad, col_index * width_part, width_part, axis=1)

    head_blocks = jnp.concatenate(
        [
            low(weight_in_grads).reshape(col_count, width_part, head_width),
            low(out_grads)
            .reshape(head_span, col_count, width_part)
            .transpose(1, 2, 0),
        ],
        axis=2,
    )
    head_blocks = col_exchange(head_blocks)
    head_blocks = lax.psum(head_blocks, "dp").astype(jnp.float32)
    query_grad = head_blocks[..., :head_span].transpose(1, 0, 2).reshape(query_weight.shape)
    key_value_grad = jnp.stack(
        [
            head_blocks[..., head_span : head_span + HEAD_SIZE],
            head_blocks[..., head_span + HEAD_SIZE : head_width],
        ]
    ).transpose(0, 2, 1, 3)
    key_value_grad = key_value_grad.reshape(key_value_matrix.shape)
    out_grad = head_blocks[..., head_width:].transpose(0, 2, 1).reshape(out_weight.shape)
    matrix_rate = 1.5 * MODEL_WIDTH ** (-0.5)
    gains_moment_new, gains_second_new, gains_new = adam_update(
        norm_gains, gain_moment, gain_second, gain_grad, 0.5, 0.0
    )
    query_moment_new, query_second_new, query_new = adam_update(
        query_weight, query_moment, query_second, query_grad, matrix_rate, weight_decay
    )
    pair_moment_new, pair_second_new, pair_new = adam_update(
        key_value_matrix,
        key_value_first_moment,
        key_value_second_moment,
        key_value_grad,
        matrix_rate,
        weight_decay,
    )
    out_moment_new, out_second_new, out_new = adam_update(
        out_weight,
        out_moment,
        out_second,
        out_grad,
        1.5 * max(1, QUERY_HEADS * HEAD_SIZE // 256) ** (-0.5),
        weight_decay,
    )
    gate_moment_new, gate_second_new, gate_new = adam_update(
        gate_up_weight, gate_up_moment, gate_up_second, grad_gate_up, matrix_rate, weight_decay
    )
    down_moment_new, down_second_new, down_new = adam_update(
        down_weight, down_moment, down_second, grad_down, 1.5 * (FF // 16) ** (-0.5), weight_decay
    )
    return (
        block_output,
        input_grad,
        gains_moment_new,
        gains_second_new,
        gains_new,
        query_moment_new,
        query_second_new,
        query_new,
        pair_moment_new,
        pair_second_new,
        pair_new,
        out_moment_new,
        out_second_new,
        out_new,
        gate_moment_new,
        gate_second_new,
        gate_new,
        down_moment_new,
        down_second_new,
        down_new,
    )


def solution(mesh):
    return jax.shard_map(
        per_device,
        mesh=mesh,
        in_specs=(
            P(("dp", "row"), "col"),
            P(("dp", "row"), "col"),
            P("dp", None),
            P("dp", None),
            P("dp"),
            P(None, "col"),
            P(None, "col"),
            P(None, "col"),
            P("col", "row"),
            P("col", "row"),
            P("col", "row"),
            P(None, "col", "row"),
            P(None, "col", "row"),
            P(None, "col", "row"),
            P("row", "col"),
            P("row", "col"),
            P("row", "col"),
            P("dp", "col", None, "row"),
            P("dp", "col", None, "row"),
            P("dp", "col", None, "row"),
            P("dp", "row", "col"),
            P("dp", "row", "col"),
            P("dp", "row", "col"),
        ),
        out_specs=(
            P(("dp", "row"), "col"),
            P(("dp", "row"), "col"),
            P(None, "col"),
            P(None, "col"),
            P(None, "col"),
            P("col", "row"),
            P("col", "row"),
            P("col", "row"),
            P(None, "col", "row"),
            P(None, "col", "row"),
            P(None, "col", "row"),
            P("row", "col"),
            P("row", "col"),
            P("row", "col"),
            P("dp", "col", None, "row"),
            P("dp", "col", None, "row"),
            P("dp", "col", None, "row"),
            P("dp", "row", "col"),
            P("dp", "row", "col"),
            P("dp", "row", "col"),
        ),
        check_vma=False,
    )
```

time: 2520 us -> 1010 us (0.40)
  waiting for transfers between devices: 1520 us -> 416 us
  other arithmetic: 337 us -> 79.9 us
  local copies, waits for them, and re-layouts: 324 us -> 154 us
  blocking collectives: 136 us -> 167 us
  matrix products: 173 us -> 143 us
    reduce_scatter x18 -> x4, waiting for transfers between devices: 1040 us -> 105 us  [the longest x2 105 us: grid_total(): return lax.psum_scatter(blocks, grid_axes, scatter_dimension=0, tiled=True)]
    gather x13 -> x0, local copies, waits for them, and re-layouts: 260 us -> none  [the longest x3 85.1 us: dispatch(): source = sorted_order[position]]
    scatter-add x8 -> x0, other arithmetic: 218 us -> none  [the longest x4 109 us: input_terms(): jax.ops.segment_sum(back_terms.reshape(-1, width_part), block_tokens.resh...]
    all_gather x12 -> x8, waiting for transfers between devices: 473 us -> 265 us  [the longest x3 57.7 us: grid_whole(): blocks = lax.all_gather(block, grid_axes, axis=0, tiled=False)]
    reshape x6 -> x15, local copies, waits for them, and re-layouts: 17.5 us -> 74.6 us  [the longest x2 35.4 us: per_device(): gate_up_grads.reshape(own_count, col_count, width_part, 2, row_count, ff_...]
    all_to_all x0 -> x5, waiting for transfers between devices: none -> 43.7 us  [the longest x1 29.6 us: col_exchange(): lax.all_to_all(blocks, 'col', split_axis=0, concat_axis=0, tiled=True)]
    dot_general x54 -> x39, matrix products: 173 us -> 143 us  [product(): return jnp.einsum(formula, left, right, preferred_element_type=jnp.float32)]
    all_gather x6 -> x1, blocking collectives: 79.4 us -> 103 us  [per_device(): gains_all = lax.all_gather(norm_gains, 'col', axis=1, tiled=True)]
  transfers between devices with their start and end apart: 31 -> 18, of which waited for: 27 -> 11; matrix products, arithmetic and copies ran while one was open for 27% -> 31% of each run, Pallas kernels for 0% -> 0%
where the time goes in v1:
time: 1010 us; the launch traced here: 999 us
  waiting for transfers between devices  416 us (41%)
  blocking collectives  167 us (17%)
  local copies, waits for them, and re-layouts  154 us (15%)
  matrix products  143 us (14%)
  other arithmetic  79.9 us (8%)
  starting transfers between devices  24.2 us (2%)
  between operations  15.4 us (2%)
    dot_general x39, matrix products, product(): return jnp.einsum(formula, left, right, preferred_element_type=jnp.float32)  143 us
    reduce_scatter x2, waiting for transfers between devices, grid_total(): return lax.psum_scatter(blocks, grid_axes, scatter_dimension=0, tiled=True)  105 us
    all_gather x1, blocking collectives, per_device(): gains_all = lax.all_gather(norm_gains, 'col', axis=1, tiled=True)  103 us
    all_gather x3, waiting for transfers between devices, grid_whole(): blocks = lax.all_gather(block, grid_axes, axis=0, tiled=False)  57.7 us
    all_gather x1, waiting for transfers between devices, per_device(): lax.all_gather(low(grad_middle), grid_axes, axis=0, tiled=True)  51.2 us
    all_gather x1, waiting for transfers between devices, per_device(): lax.all_gather(weight_in_here, grid_axes, axis=0, tiled=False)  49.7 us
    all_gather x1, waiting for transfers between devices, per_device(): context_all = lax.all_gather(context, grid_axes, axis=1, tiled=True)  43.5 us
    all_gather x1, waiting for transfers between devices, per_device(): gate_up_mine = lax.all_gather(gate_up_mine, 'dp', axis=0, tiled=True)  39 us
  transfers between devices with their start and end apart: 18, of which 11 were waited for; matrix products, arithmetic and copies ran while one was open for 31% of the time, Pallas kernels for 0%

profile of v1, /device:TPU:0, one launch (start us, length us, event | category | flops | bytes accessed | tf_op | source)
XLA Modules:
  0.0 998.8 jit_solution(7719856964529386696)
XLA Ops:
  32.4 103.0 %all_gather.41 = f32[2,1024]{1,0:T(2,128)S(1)} all-gather(f32[2,256]{1,0:T(2,128)S(1)} %copy-done.81), channel_id=1, replica_groups=mesh['dp'=4,'row'=2,'col'=4] {'col'}, dimensions={1}, use_global_device_ids=true | all-gather | bytes 10240 | tf_op jit(solution)/shard_map/all_gather | solution.py:218
  152.5 49.7 %all-gather.23.cloned.1.call-done = bf16[32,256,256]{2,1,0:T(8,128)(2,1)} async-done(((bf16[4,256,256]{2,1,0:T(8,128)(2,1)}), bf16[32,256,256]{2,1,0:T(8,128)(2,1)}) %all-gather.23.cloned.1.call-update) | async-done | bytes 4194320 | tf_op jit(solution)/shard_map/all_gather | solution.py:188
  244.0 8.5 all-gather.25.cloned.1.call-done
  264.2 49.2 %all-gather.27.cloned.1.call-done = bf16[6144,256]{1,0:T(8,128)(2,1)} async-done(((bf16[768,256]{1,0:T(8,128)(2,1)}), bf16[6144,256]{1,0:T(8,128)(2,1)}) %all-gather.27.cloned.1.call-update) | async-done | bytes 3145744 | tf_op jit(solution)/shard_map/all_gather | solution.py:46
  321.8 9.7 multiply_convert_fusion
  331.5 43.5 %all-gather.13.cloned.1.call-done = bf16[1536,1024]{0,1:T(8,128)(2,1)} async-done(((bf16[1536,128]{0,1:T(8,128)(2,1)}), bf16[1536,1024]{0,1:T(8,128)(2,1)}) %all-gather.13.cloned.1.call-update) | async-done | bytes 3145744 | tf_op jit(solution)/shard_map/all_gather | solution.py:251
  386.5 8.5 fusion.28
  395.0 39.0 %all-gather.15.cloned.1.call-done = bf16[4,1024,1024]{2,1,0:T(8,128)(2,1)} async-done(((bf16[1,1024,1024]{2,1,0:T(8,128)(2,1)}), bf16[4,1024,1024]{2,1,0:T(8,128)(2,1)}) %all-gather.15.cloned.1.call-update) | async-done | bytes 8388624 | tf_op jit(solution)/shard_map/all_gather | solution.py:215
  433.9 12.4 %fusion.121 = f32[4,480,1024]{2,1,0:T(8,128)} fusion(bf16[4,480,1024]{2,1,0:T(8,128)(2,1)} %fusion.28, bf16[4,1024,1024]{2,1,0:T(8,128)(2,1)} %all-gather.15.cloned.1.call-done), kind=kOutput, calls=%fused_computation.228 | convolution fusion | flops 4026531840 | bytes 20185088 | tf_op jit(solution)/shard_map/isd,idf->isf/dot_general | solution.py:31
  446.3 24.3 %all-gather.17.cloned.1.call-done = bf16[4,512,1024]{2,1,0:T(8,128)(2,1)} async-done(((bf16[1,512,1024]{2,1,0:T(8,128)(2,1)}), bf16[4,512,1024]{2,1,0:T(8,128)(2,1)}) %all-gather.17.cloned.1.call-update) | async-done | bytes 4194320 | tf_op jit(solution)/shard_map/all_gather | solution.py:216
  470.6 11.9 %multiply_convert_fusion.8 = (bf16[4,480,512]{2,1,0:T(8,128)(2,1)}, bf16[4,480,512]{2,1,0:T(8,128)(2,1)}, bf16[4,480,512]{2,1,0:T(8,128)(2,1)}) fusion(f32[4,480,1024]{2,1,0:T(8,128)} %fusion.121, bf16[4,480,1024]{2,1,0:T(8,128)(2,1)} %multiply_convert_fusion, bf16[4,512,1024]{2,1,0:T(8,128)(2,1)} %all-gather.17.cloned.1.call-done), kind=kOutput, calls=%fused_computation.38 | convolution fusion | flops 2028994560 | bytes 21889024 | tf_op jit(solution)/shard_map/isd,ifd->isf/dot_general | solution.py:31
  482.5 15.8 %bitcast_convert_fusion = bf16[1536,1024]{1,0:T(8,128)(2,1)} fusion(bf16[4,1024,1024]{2,1,0:T(8,128)(2,1)} %all-gather.15.cloned.1.call-done, s32[4,1536]{1,0:T(4,128)S(1)} %fusion.38, bf16[4,480,512]{2,1,0:T(8,128)(2,1)} %get-tuple-element.145, bf16[4,480,512]{2,1,0:T(8,128)(2,1)} %get-tuple-element.144), kind=kOutput, calls=%fused_computation.11 | convolution fusion | flops 10080681984 | bytes 15491072 | tf_op jit(solution)/shard_map/ist,isd->td/dot_general | solution.py:31
  521.0 51.8 %reduce-scatter.7.cloned.1.call-done = bf16[192,1024]{1,0:T(8,128)(2,1)} async-done(((bf16[1536,1024]{1,0:T(8,128)(2,1)}), bf16[192,1024]{1,0:T(8,128)(2,1)}) %reduce-scatter.7.cloned.1.call-update) | async-done | bytes 393232 | tf_op jit(solution)/shard_map/reduce_scatter | solution.py:60
  577.6 10.8 %convolution_convert_fusion = bf16[4,1024,1024]{2,1,0:T(8,128)(2,1)} fusion(bf16[4,480,1024]{2,1,0:T(8,128)(2,1)} %fusion.28, bf16[4,480,512]{2,1,0:T(8,128)(2,1)} %get-tuple-element.145, bf16[4,480,512]{2,1,0:T(8,128)(2,1)S(1)} %copy-done.86), kind=kOutput, calls=%fused_computation.10 | convolution fusion | flops 4038590464 | bytes 16252928 | tf_op jit(solution)/shard_map/isd,isf->idf/dot_general | solution.py:31
  588.4 14.5 %reshape.334 = bf16[4,4,256,2,2,256]{5,4,3,2,1,0:T(2,128)(2,1)} reshape(bf16[4,1024,1024]{2,1,0:T(8,128)(2,1)} %convolution_convert_fusion) | data formatting | bytes 16777216 | tf_op jit(solution)/shard_map/reshape | solution.py:279
  602.9 20.9 %copy.243 = bf16[4,4,256,2,2,256]{2,5,3,1,4,0:T(8,128)(2,1)} copy(bf16[4,4,256,2,2,256]{5,4,3,2,1,0:T(2,128)(2,1)} %reshape.334) | data formatting | bytes 16777216 | tf_op jit(solution)/shard_map/reshape | solution.py:279
  625.4 11.8 %bitcast_convert_fusion.1 = bf16[1536,1024]{1,0:T(8,128)(2,1)} fusion(f32[4,480]{1,0:T(4,128)S(1)} %select_reduce_fusion, s32[4,1536]{1,0:T(4,128)S(1)} %fusion.38, bf16[4,480,512]{2,1,0:T(8,128)(2,1)S(1)} %copy-done.85, bf16[4,512,1024]{2,1,0:T(8,128)(2,1)} %all-gather.17.cloned.1.call-done), kind=kOutput, calls=%fused_computation.12 | convolution fusion | flops 8061517824 | bytes 9338368 | tf_op jit(solution)/shard_map/ist,isd->td/dot_general | solution.py:31
  648.8 51.2 %all-gather.19.cloned.1.call-done = bf16[1536,1024]{1,0:T(8,128)(2,1)} async-done(((bf16[192,1024]{1,0:T(8,128)(2,1)}), bf16[1536,1024]{1,0:T(8,128)(2,1)}) %all-gather.19.cloned.1.call-update) | async-done | bytes 3145744 | tf_op jit(solution)/shard_map/all_gather | solution.py:300
  764.7 14.2 %all-to-all-done.1 = bf16[8,192,256]{2,1,0:T(8,128)(2,1)} async-done(((bf16[8,192,256]{2,1,0:T(8,128)(2,1)}), bf16[8,192,256]{2,1,0:T(8,128)(2,1)}, u32[]{:S(2)}, u32[]{:S(2)}) %all-to-all-start.1) | async-done | bytes 786464 | tf_op jit(solution)/shard_map/all_to_all | solution.py:52
  789.2 29.6 %all-to-all-done.3 = bf16[4,256,384]{1,2,0:T(8,128)(2,1)S(1)} async-done(((bf16[4,256,384]{1,2,0:T(8,128)(2,1)}), bf16[4,256,384]{1,2,0:T(8,128)(2,1)S(1)}, u32[]{:S(2)}, u32[]{:S(2)}) %all-to-all-start.3) | async-done | bytes 786464 | tf_op jit(solution)/shard_map/all_to_all | solution.py:56
  818.8 25.1 %all_to_all.30 = f32[4,192,256]{2,1,0:T(8,128)} all-to-all(f32[4,192,256]{2,1,0:T(8,128)S(1)} %bitcast.285), channel_id=1, replica_groups=mesh['dp'=4,'row'=2,'col'=4] {'col'}, dimensions={0} | all-to-all | bytes 1572864 | tf_op jit(solution)/shard_map/all_to_all | solution.py:56
  850.6 53.3 %reduce-scatter.5.cloned.1.call-done = bf16[768,256]{1,0:T(8,128)(2,1)} async-done(((bf16[6144,256]{1,0:T(8,128)(2,1)}), bf16[768,256]{1,0:T(8,128)(2,1)}) %reduce-scatter.5.cloned.1.call-update) | async-done | bytes 393232 | tf_op jit(solution)/shard_map/reduce_scatter | solution.py:60
  912.9 38.4 %psum.14 = f32[2,1024]{1,0:T(2,128)S(1)} all-reduce(f32[2,1024]{1,0:T(2,128)S(1)} %pad_maximum_fusion.9), channel_id=1, replica_groups=mesh['dp'=4,'row'=2,'col'=4] {'dp','row','col'}, use_global_device_ids=true, to_apply=%region_23.24 | all-reduce | flops 2048 | bytes 16384 | tf_op jit(solution)/shard_map/psum | solution.py:326
  973.2 17.9 %multiply_subtract_fusion = (f32[8,256,2,256]{3,2,1,0:T(2,128)}, f32[8,256,2,256]{3,2,1,0:T(2,128)}, f32[8,256,2,256]{3,2,1,0:T(2,128)}) fusion(f32[8,256,2,256]{3,2,1,0:T(2,128)} %param.40, f32[8,256,2,256]{3,2,1,0:T(2,128)} %copy.245, f32[8,256,2,256]{3,2,1,0:T(2,128)} %param.42, f32[8,256,2,256]{3,2,1,0:T(2,128)} %param.41), kind=kLoop, calls=%fused_computation.30 | loop fusion | flops 14680064 | bytes 29360128 | tf_op jit(solution)/shard_map/sub | solution.py:130
  (359 shorter events, 268.3 us)
Async XLA Ops:
  7.2 132.7 %all-gather.21.cloned.1.call-start = ((), (), s32[]{:S(2)}) async-start(), calls=%async_computation.19 | async-start | bytes 3538944 | tf_op jit(solution)/shard_map/all_gather | solution.py:46
  7.9 194.2 %all-gather.23.cloned.1.call-start = ((), (), s32[]{:S(2)}) async-start(), calls=%async_computation.20 | async-start | bytes 4718592 | tf_op jit(solution)/shard_map/all_gather | solution.py:188
  11.7 240.7 %all-gather.25.cloned.1.call-start = ((), (), s32[]{:S(2)}) async-start(), calls=%async_computation.21 | async-start | bytes 2359296 | tf_op jit(solution)/shard_map/all_gather | solution.py:46
  24.4 193.8 %all-to-all-start = ((bf16[8,1,256,768]{3,2,1,0:T(8,128)(2,1)}), bf16[8,1,256,768]{3,2,1,0:T(8,128)(2,1)}, u32[]{:S(2)}, u32[]{:S(2)}) async-start(bf16[8,1,256,768]{3,2,1,0:T(8,128)(2,1)} %pad_maximum_fusion.1), calls=%async_computation | async-start | bytes 6291456 | tf_op jit(solution)/shard_map/all_to_all | solution.py:52
  31.7 281.7 %all-gather.27.cloned.1.call-start = ((), (), s32[]{:S(2)}) async-start(), calls=%async_computation.22 | async-start | bytes 3538944 | tf_op jit(solution)/shard_map/all_gather | solution.py:46
  32.2 342.8 %all-gather.13.cloned.1.call-start = ((), (), s32[]{:S(2)}) async-start(), calls=%async_computation.10 | async-start | bytes 3538944 | tf_op jit(solution)/shard_map/all_gather | solution.py:251
  139.9 74.5 %copy-start.13 = (pred[384,768]{1,0:T(8,128)(4,1)}, pred[384,768]{1,0:T(8,128)(4,1)S(1)}, u32[]{:S(2)}) copy-start(pred[384,768]{1,0:T(8,128)(4,1)S(1)} %compare_and_fusion.1) | copy-start | bytes 884740
  218.1 215.8 %all-gather.15.cloned.1.call-start = ((), (), s32[]{:S(2)}) async-start(), calls=%async_computation.11 | async-start | bytes 10485760 | tf_op jit(solution)/shard_map/all_gather | solution.py:215
  235.3 235.3 %all-gather.17.cloned.1.call-start = ((), (), s32[]{:S(2)}) async-start(), calls=%async_computation.12 | async-start | bytes 5242880 | tf_op jit(solution)/shard_map/all_gather | solution.py:216
  241.2 331.6 %reduce-scatter.7.cloned.1.call-start = ((), (), s32[]{:S(2)}) async-start(), calls=%async_computation.14 | async-start | bytes 3538944 | tf_op jit(solution)/shard_map/reduce_scatter | solution.py:60
  498.4 145.7 %reduce-scatter.11.cloned.1.call-start = ((), (), s32[]{:S(2)}) async-start(), calls=%async_computation.18 | async-start | bytes 5242880 | tf_op jit(solution)/shard_map/reduce_scatter | solution.py:80
  518.4 181.5 %all-gather.19.cloned.1.call-start = ((), (), s32[]{:S(2)}) async-start(), calls=%async_computation.15 | async-start | bytes 3538944 | tf_op jit(solution)/shard_map/all_gather | solution.py:300
  520.9 56.7 %copy-start.86 = (bf16[4,480,512]{2,1,0:T(8,128)(2,1)S(1)}, bf16[4,480,512]{2,1,0:T(8,128)(2,1)}, u32[]{:S(2)}) copy-start(bf16[4,480,512]{2,1,0:T(8,128)(2,1)} %get-tuple-element.144) | copy-start | bytes 5898244
  520.9 67.5 %copy-start.68 = (f32[192]{0:T(256)}, f32[192]{0:T(256)S(1)}, u32[]{:S(2)}) copy-start(f32[192]{0:T(256)S(1)} %dynamic-slice.3) | copy-start | bytes 2308
  521.0 67.5 %copy-start.76 = (f32[192,1]{0,1:T(1,128)}, f32[192,1]{0,1:T(1,128)S(1)}, u32[]{:S(2)}) copy-start(f32[192,1]{0,1:T(1,128)S(1)} %multiply_multiply_fusion.6) | copy-start | bytes 2308
  577.3 266.5 %reduce-scatter.9.cloned.1.call-start = ((), (), s32[]{:S(2)}) async-start(), calls=%async_computation.17 | async-start | bytes 10485760 | tf_op jit(solution)/shard_map/reduce_scatter | solution.py:80
  623.9 280.0 %reduce-scatter.5.cloned.1.call-start = ((), (), s32[]{:S(2)}) async-start(), calls=%async_computation.13 | async-start | bytes 3538944 | tf_op jit(solution)/shard_map/reduce_scatter | solution.py:60
  644.1 109.2 %all-to-all-start.5 = ((bf16[8,1,256,256]{3,2,1,0:T(8,128)(2,1)}), bf16[8,1,256,256]{3,2,1,0:T(8,128)(2,1)}, u32[]{:S(2)}, u32[]{:S(2)}) async-start(bf16[8,1,256,256]{3,2,1,0:T(8,128)(2,1)} %bitcast.310), calls=%async_computation.9 | async-start | bytes 2097152 | tf_op jit(solution)/shard_map/all_to_all | solution.py:52
  648.8 54.4 %copy-start.2 = (f32[2,384,1152]{2,1,0:T(8,128)S(1)}, f32[2,384,1152]{2,1,0:T(8,128)}, u32[]{:S(2)}) copy-start(f32[2,384,1152]{2,1,0:T(8,128)} %copy-done.1) | copy-start | bytes 10616836
  753.4 25.5 %all-to-all-start.1 = ((bf16[8,192,256]{2,1,0:T(8,128)(2,1)}), bf16[8,192,256]{2,1,0:T(8,128)(2,1)}, u32[]{:S(2)}, u32[]{:S(2)}) async-start(bf16[8,192,256]{2,1,0:T(8,128)(2,1)} %pad_maximum_fusion.5), calls=%async_computation.3 | async-start | bytes 1572864 | tf_op jit(solution)/shard_map/all_to_all | solution.py:52
  778.9 39.9 %all-to-all-start.3 = ((bf16[4,256,384]{1,2,0:T(8,128)(2,1)}), bf16[4,256,384]{1,2,0:T(8,128)(2,1)S(1)}, u32[]{:S(2)}, u32[]{:S(2)}) async-start(bf16[4,256,384]{1,2,0:T(8,128)(2,1)} %pad_maximum_fusion.6), calls=%async_computation.5 | async-start | bytes 1572864 | tf_op jit(solution)/shard_map/all_to_all | solution.py:56
  789.2 58.3 %copy-start.51 = (f32[2,256,256]{2,1,0:T(8,128)S(1)}, f32[2,256,256]{2,1,0:T(8,128)}, u32[]{:S(2)}) copy-start(f32[2,256,256]{2,1,0:T(8,128)} %param.36) | copy-start | bytes 1572868
  843.9 125.4 %all-to-all-start.4 = ((bf16[8,1,256,512]{2,3,1,0:T(8,128)(2,1)}), bf16[8,1,256,512]{2,3,1,0:T(8,128)(2,1)S(1)}, u32[]{:S(2)}, u32[]{:S(2)}) async-start(bf16[8,1,256,512]{2,3,1,0:T(8,128)(2,1)} %bitcast.287), calls=%async_computation.7 | async-start | bytes 4194304 | tf_op jit(solution)/shard_map/all_to_all | solution.py:52
  847.5 104.5 %all-reduce.8.cloned.1.call-start = ((), (), s32[]{:S(2)}) async-start(), calls=%async_computation.16 | async-start | bytes 1572864 | tf_op jit(solution)/shard_map/psum | solution.py:339
  (85 other events, 570.2 us)
Sparse Core Ops, SparseCore 0:
  10.1 117.6 all-gather.20
  130.6 71.5 all-gather.22
  204.9 47.5 all-gather.24
  254.4 58.9 all-gather.26
  315.9 59.0 all-gather.12
  377.0 56.9 all-gather.14
  436.1 34.4 all-gather.16
  498.5 74.2 reduce-scatter.6
  575.9 43.5 reduce-scatter.10
  622.3 77.6 all-gather.18
  702.7 70.6 reduce-scatter.8
  777.5 126.3 reduce-scatter.4
  906.8 32.3 all-reduce.7

commit v2 on v1

--- a/solution.py
+++ b/solution.py
@@ -40,10 +40,18 @@
     )
 
 
-def grid_whole(block):
+def copies(block, axes):
+    count = 1
+    for axis in axes:
+        count *= lax.axis_size(axis)
+    equal = jnp.broadcast_to(block[None], (count, *block.shape))
+    return lax.all_to_all(equal, axes, split_axis=0, concat_axis=0, tiled=True)
+
+
+def grid_whole(block, gather):
     row_count, col_count = lax.axis_size("row"), lax.axis_size("col")
     tokens, width = block.shape
-    blocks = lax.all_gather(block, grid_axes, axis=0, tiled=False)
+    blocks = gather(block)
     blocks = blocks.reshape(row_count, col_count, tokens, width).transpose(0, 2, 1, 3)
     return blocks.reshape(row_count * tokens, col_count * width)
 
@@ -54,6 +62,14 @@
 
 def col_exchange(blocks):
     return lax.all_to_all(blocks, "col", split_axis=0, concat_axis=0, tiled=True)
+
+
+def gathered(block):
+    return lax.all_gather(block, grid_axes, axis=0, tiled=False)
+
+
+def copied(block):
+    return copies(block, grid_axes)
 
 
 def grid_total(blocks):
@@ -77,7 +93,10 @@
 def expert_blocks(grads, experts_here):
     grid = grads.shape[1]
     if experts_here % grid == 0:
-        mine = lax.psum_scatter(grads, "dp", scatter_dimension=0, tiled=True)
+        dp_count = lax.axis_size("dp")
+        parts = lax.all_to_all(grads, "dp", split_axis=0, concat_axis=0, tiled=True)
+        parts = parts.reshape(dp_count, -1, *grads.shape[1:])
+        mine = low(jnp.sum(parts.astype(jnp.float32), axis=0))
         mine = grid_exchange(mine.swapaxes(0, 1)).swapaxes(0, 1)
         return mine.reshape(experts_here, *grads.shape[2:])
     every = grid_exchange(grads.swapaxes(0, 1)).swapaxes(0, 1)
@@ -184,15 +203,9 @@
         )
     ).transpose(1, 0, 2)
     head_width = weight_in_here.shape[2]
-    inputs_all = grid_whole(inputs)
-    weight_in_all = lax.all_gather(weight_in_here, grid_axes, axis=0, tiled=False)
-    weight_in_all = (
-        weight_in_all.reshape(row_count, col_count, heads_here, width_part, head_width)
-        .transpose(0, 2, 1, 3, 4)
-        .reshape(grid, MODEL_WIDTH, head_width)
-    )
-    weight_in = lax.dynamic_index_in_dim(weight_in_all, place, axis=0, keepdims=False)
-    out_all = grid_whole(low(out_weight))
+    inputs_all = grid_whole(inputs, gathered)
+    weight_in = col_exchange(weight_in_here).reshape(MODEL_WIDTH, head_width)
+    out_all = grid_whole(low(out_weight), copied)
     expert_weights = low(
         jnp.concatenate(
             [gate_up_weight.reshape(experts_here, width_part, 2 * ff_part), down_weight], axis=2
@@ -201,8 +214,8 @@
     expert_weights, spread = whole_experts(expert_weights)
     gate_up_mine = (
         expert_weights[..., : 2 * ff_part]
-        .reshape(-1, row_count, col_count * width_part, 2, ff_part)
-        .transpose(0, 2, 3, 1, 4)
+        .reshape(-1, row_count, col_count * width_part, 2 * ff_part)
+        .transpose(0, 2, 1, 3)
         .reshape(-1, MODEL_WIDTH, 2 * FF)
     )
     down_mine = (
@@ -211,11 +224,12 @@
         .transpose(0, 1, 3, 2, 4)
         .reshape(-1, FF, MODEL_WIDTH)
     )
+    inputs_all, gate_up_mine = lax.optimization_barrier((inputs_all, gate_up_mine))
     if spread:
         gate_up_mine = lax.all_gather(gate_up_mine, "dp", axis=0, tiled=True)
         down_mine = lax.all_gather(down_mine, "dp", axis=0, tiled=True)
-    cotangent_all = grid_whole(cotangent)
-    gains_all = lax.all_gather(norm_gains, "col", axis=1, tiled=True)
+    cotangent_all = grid_whole(cotangent, copied)
+    gains_all = copies(norm_gains, ("col",)).transpose(1, 0, 2).reshape(2, MODEL_WIDTH)
 
     own_ids = jnp.arange(own_count, dtype=jnp.int32) * grid + place
     named = routes[:, :, None] == own_ids[None, None, :]
@@ -255,30 +269,46 @@
 
     slot_inputs = low(product("ist,td->isd", pick, normed_two))
     gate_up = product("isd,idf->isf", slot_inputs, gate_up_mine)
-    gate_part, up_part = gate_up[..., :FF], gate_up[..., FF:]
+    gate_part = jnp.concatenate(
+        [gate_up[..., 2 * r * ff_part : (2 * r + 1) * ff_part] for r in range(row_count)], axis=2
+    )
+    up_part = jnp.concatenate(
+        [gate_up[..., (2 * r + 1) * ff_part : (2 * r + 2) * ff_part] for r in range(row_count)],
+        axis=2,
+    )
     hidden = low(jax.nn.silu(gate_part) * up_part)
     expert_out = low(product("isf,ifd->isd", hidden, down_mine) * slot_weights)
     mixture = low(product("ist,isd->td", pick, expert_out))
-    mixture = grid_total(grid_split(mixture).reshape(-1, width_part))
+    mixture = grid_exchange(grid_split(mixture))
+    mixture = jnp.sum(mixture.astype(jnp.float32), axis=0)
     middle_here = lax.dynamic_slice(
         middle, (row_index * half_tokens, col_index * width_part), (half_tokens, width_part)
     )
-    block_output = low(middle_here + mixture.astype(jnp.float32))
+    block_output = low(middle_here + mixture)
 
     grad_slots = low(product("ist,td->isd", pick, cotangent_all) * slot_weights)
     grad_hidden = product("isd,ifd->isf", grad_slots, down_mine)
     sigmoid_gate = jax.nn.sigmoid(gate_part)
     grad_gate = grad_hidden * up_part * sigmoid_gate * (1.0 + gate_part * (1.0 - sigmoid_gate))
     grad_up = grad_hidden * gate_part * sigmoid_gate
-    grad_pair = low(jnp.concatenate([grad_gate, grad_up], axis=2))
+    grad_pair = low(
+        jnp.concatenate(
+            [
+                side[..., r * ff_part : (r + 1) * ff_part]
+                for r in range(row_count)
+                for side in (grad_gate, grad_up)
+            ],
+            axis=2,
+        )
+    )
     back_slots = low(product("isf,idf->isd", grad_pair, gate_up_mine))
     grad_normed_two = low(product("ist,isd->td", pick, back_slots))
     grad_normed_two = grid_total(grad_normed_two).astype(jnp.float32)
     down_grads = low(product("isf,isd->ifd", hidden, grad_slots))
     gate_up_grads = low(product("isd,isf->idf", slot_inputs, grad_pair))
     gate_up_grads = gate_up_grads.reshape(
-        own_count, col_count, width_part, 2, row_count, ff_part
-    ).transpose(0, 4, 1, 2, 3, 5)
+        own_count, col_count, width_part, row_count, 2 * ff_part
+    ).transpose(0, 3, 1, 2, 4)
     gate_up_grads = gate_up_grads.reshape(own_count, grid, width_part, 2 * ff_part)
     down_grads = down_grads.reshape(
         own_count, row_count, ff_part, col_count, width_part
@@ -299,6 +329,13 @@
     grad_gain_two = jnp.sum(grad_normed_two * middle_part * scale_part, axis=0)
     grad_middle_all = lax.all_gather(low(grad_middle), grid_axes, axis=0, tiled=True)
 
+    weight_in_here, grad_middle = lax.optimization_barrier((weight_in_here, grad_middle))
+    weight_in_all = lax.all_gather(weight_in_here, grid_axes, axis=0, tiled=False)
+    weight_in_all = (
+        weight_in_all.reshape(row_count, col_count, heads_here, width_part, head_width)
+        .transpose(0, 2, 1, 3, 4)
+        .reshape(grid, MODEL_WIDTH, head_width)
+    )
     out_mine = own_rows(out_all, place, head_span)
     grad_context = low(product("td,hd->th", grad_middle_all, out_mine))
     out_grads = product("th,td->hd", context, grad_middle_all)
@@ -323,8 +360,18 @@
     grad_gain_one = jnp.sum(grad_normed * residual_part * scale_part, axis=0)
     input_grad = input_grad.reshape(part_tokens, col_count, width_part).transpose(1, 0, 2)
     input_grad = col_exchange(input_grad).reshape(half_tokens, width_part)
-    gain_grad = lax.psum(jnp.stack([grad_gain_one, grad_gain_two]), ("dp", "row", "col"))
-    gain_grad = lax.dynamic_slice_in_dim(gain_grad, col_index * width_part, width_part, axis=1)
+    gain_grad = jnp.stack([grad_gain_one, grad_gain_two]).reshape(2, col_count, width_part)
+    gain_grad = jnp.broadcast_to(
+        gain_grad.transpose(1, 0, 2), (lax.axis_size("dp") * row_count, col_count, 2, width_part)
+    )
+    gain_grad = lax.all_to_all(
+        gain_grad.reshape(-1, 2, width_part),
+        ("dp", "row", "col"),
+        split_axis=0,
+        concat_axis=0,
+        tiled=True,
+    )
+    gain_grad = jnp.sum(gain_grad, axis=0)
 
     head_blocks = jnp.concatenate(
         [
@@ -336,7 +383,10 @@
         axis=2,
     )
     head_blocks = col_exchange(head_blocks)
-    head_blocks = lax.psum(head_blocks, "dp").astype(jnp.float32)
+    if lax.axis_size("dp") <= 4:
+        head_blocks = jnp.sum(copies(head_blocks, ("dp",)).astype(jnp.float32), axis=0)
+    else:
+        head_blocks = lax.psum(head_blocks, "dp").astype(jnp.float32)
     query_grad = head_blocks[..., :head_span].transpose(1, 0, 2).reshape(query_weight.shape)
     key_value_grad = jnp.stack(
         [

time: 1010 us -> 949 us (0.940)
  blocking collectives: 167 us -> 89.9 us
  starting transfers between devices: 24.2 us -> 64.5 us
  waiting for transfers between devices: 416 us -> 402 us
    all_to_all x0 -> x6, waiting for transfers between devices: none -> 178 us  [the longest x2 95.1 us: expert_blocks(): parts = lax.all_to_all(grads, 'dp', split_axis=0, concat_axis=0, tiled=True)]
    all_to_all x4 -> x5, waiting for transfers between devices: 14.2 us -> 120 us  [grid_exchange(): lax.all_to_all(blocks, grid_axes, split_axis=0, concat_axis=0, tiled=True)]
    reduce_scatter x2 -> x1, waiting for transfers between devices: 105 us -> 1.07 us  [grid_total(): return lax.psum_scatter(blocks, grid_axes, scatter_dimension=0, tiled=True)]
    all_gather x1 -> x0, blocking collectives: 103 us -> none  [per_device(): gains_all = lax.all_gather(norm_gains, 'col', axis=1, tiled=True)]
    all_to_all x1, blocking collectives: 25.1 us -> 89.9 us  [copies(): return lax.all_to_all(equal, axes, split_axis=0, concat_axis=0, tiled=True)]
    all_gather x1, waiting for transfers between devices: 51.2 us -> 0.01 us  [per_device(): lax.all_gather(low(grad_middle), grid_axes, axis=0, tiled=True)]
    all_gather x1, waiting for transfers between devices: 49.7 us -> 0.01 us  [per_device(): lax.all_gather(weight_in_here, grid_axes, axis=0, tiled=False)]
    all_gather x1, waiting for transfers between devices: 43.5 us -> 0.02 us  [per_device(): context_all = lax.all_gather(context, grid_axes, axis=1, tiled=True)]
  transfers between devices with their start and end apart: 18 -> 21, of which waited for: 11 -> 14; matrix products, arithmetic and copies ran while one was open for 31% -> 30% of each run, Pallas kernels for 0% -> 0%
where the time goes in v2:
time: 949 us; the launch traced here: 939 us
  waiting for transfers between devices  402 us (42%)
  local copies, waits for them, and re-layouts  150 us (16%)
  matrix products  133 us (14%)
  blocking collectives  89.9 us (9%)
  other arithmetic  83.5 us (9%)
  starting transfers between devices  64.5 us (7%)
  between operations  16 us (2%)
    dot_general x39, matrix products, product(): return jnp.einsum(formula, left, right, preferred_element_type=jnp.float32)  133 us
    all_to_all x5, waiting for transfers between devices, grid_exchange(): lax.all_to_all(blocks, grid_axes, split_axis=0, concat_axis=0, tiled=True)  120 us
    all_gather x1, waiting for transfers between devices, gathered(): return lax.all_gather(block, grid_axes, axis=0, tiled=False)  95.9 us
    all_to_all x2, waiting for transfers between devices, expert_blocks(): parts = lax.all_to_all(grads, 'dp', split_axis=0, concat_axis=0, tiled=True)  95.1 us
    all_to_all x1, blocking collectives, copies(): return lax.all_to_all(equal, axes, split_axis=0, concat_axis=0, tiled=True)  89.9 us
    all_to_all x3, waiting for transfers between devices, copies(): return lax.all_to_all(equal, axes, split_axis=0, concat_axis=0, tiled=True)  78.6 us
    unnamed x170, local copies, waits for them, and re-layouts  36.7 us
    sub x6, other arithmetic, adam_update(): weight - step_size * moment_new / denominator  28.6 us
  transfers between devices with their start and end apart: 21, of which 14 were waited for; matrix products, arithmetic and copies ran while one was open for 30% of the time, Pallas kernels for 0%

profile of v2, /device:TPU:0, one launch (start us, length us, event | category | flops | bytes accessed | tf_op | source)
XLA Modules:
  0.0 939.2 jit_solution(11335036645316727394)
XLA Ops:
  8.5 6.3 all-to-all-start.1
  47.4 95.9 %all-gather.17.cloned.1.call-done = bf16[6144,256]{1,0:T(8,128)(2,1)} async-done(((bf16[768,256]{1,0:T(8,128)(2,1)}), bf16[6144,256]{1,0:T(8,128)(2,1)}) %all-gather.17.cloned.1.call-update) | async-done | bytes 3145744 | tf_op jit(solution)/shard_map/all_gather | solution.py:68
  172.9 89.9 %all_to_all.75 = bf16[8,512,256]{2,1,0:T(8,128)(2,1)} all-to-all(bf16[8,512,256]{2,1,0:T(8,128)(2,1)S(1)} %broadcast_in_dim.87), channel_id=1, replica_groups=mesh['dp'=4,'row'=2,'col'=4] {'row','col'}, dimensions={0} | all-to-all | bytes 4194304 | tf_op jit(solution)/shard_map/all_to_all | solution.py:48
  280.8 58.3 %all-to-all-done.5 = bf16[8,768,256]{2,1,0:T(8,128)(2,1)S(1)} async-done(((bf16[8,768,256]{2,1,0:T(8,128)(2,1)}), bf16[8,768,256]{2,1,0:T(8,128)(2,1)S(1)}, u32[]{:S(2)}, u32[]{:S(2)}) %all-to-all-start.5) | async-done | bytes 3145760 | tf_op jit(solution)/shard_map/all_to_all | solution.py:48
  349.0 9.8 %multiply_convert_fusion = bf16[4,480,1024]{2,1,0:T(8,128)(2,1)} fusion(f32[4,480]{1,0:T(4,128)S(1)} %select_reduce_fusion, bf16[1536,1024,1]{1,0,2:T(8,128)(2,1)} %reshape.366, s32[4,1536]{1,0:T(4,128)S(1)} %fusion.35), kind=kOutput, calls=%fused_computation.8 | convolution fusion | flops 6046679040 | bytes 7110144 | tf_op jit(solution)/shard_map/ist,td->isd/dot_general | solution.py:31
  358.8 7.4 multiply_reduce_fusion
  368.9 8.1 fusion.25
  376.9 7.8 fusion.117
  388.3 9.7 %multiply_convert_fusion.7 = (bf16[4,480,512]{2,1,0:T(8,128)(2,1)}, bf16[4,480,512]{2,1,0:T(8,128)(2,1)S(1)}, bf16[4,480,512]{2,1,0:T(8,128)(2,1)}) fusion(f32[4,480,256]{2,1,0:T(8,128)} %get-tuple-element.196, f32[4,480,256]{2,1,0:T(8,128)} %get-tuple-element.197, f32[4,480,256]{2,1,0:T(8,128)} %get-tuple-element.198, ...), kind=kOutput, calls=%fused_computation.41 | convolution fusion | flops 2030960640 | bytes 21889024 | tf_op jit(solution)/shard_map/isd,ifd->isf/dot_general | solution.py:31
  403.7 7.8 reshape.348
  425.5 15.6 %bitcast_convert_fusion = bf16[1536,1024]{1,0:T(8,128)(2,1)} fusion(bf16[4,1024,1024]{2,1,0:T(8,128)(2,1)} %all-gather.11.cloned.1.call-done, s32[4,1536]{1,0:T(4,128)S(1)} %fusion.35, bf16[4,480,256]{2,1,0:T(8,128)(2,1)} %get-tuple-element.234, bf16[4,480,256]{2,1,0:T(8,128)(2,1)} %get-tuple-element.200, bf16[4,480,256]{2,1,0:T(8,128)(2,1)} %get-tuple-element.235, ...), kind=kOutput, calls=%fused_computation.11 | convolution fusion | flops 10088546304 | bytes 15491072 | tf_op jit(solution)/shard_map/ist,isd->td/dot_general | solution.py:31
  441.1 28.5 %all-to-all-done.13 = bf16[4,8,256,256]{3,2,1,0:T(8,128)(2,1)} async-done(((bf16[4,8,256,256]{3,2,1,0:T(8,128)(2,1)}), bf16[4,8,256,256]{3,2,1,0:T(8,128)(2,1)}, u32[]{:S(2)}, u32[]{:S(2)}) %all-to-all-start.13) | async-done | bytes 4194336 | tf_op jit(solution)/shard_map/all_to_all | solution.py:97
  478.4 11.2 %convolution_convert_fusion = bf16[4,1024,1024]{2,1,0:T(8,128)(2,1)} fusion(bf16[4,480,1024]{2,1,0:T(8,128)(2,1)} %fusion.25, bf16[4,480,256]{2,1,0:T(8,128)(2,1)} %get-tuple-element.234, bf16[4,480,256]{2,1,0:T(8,128)(2,1)} %get-tuple-element.200, bf16[4,480,256]{2,1,0:T(8,128)(2,1)} %get-tuple-element.235, bf16[4,480,256]{2,1,0:T(8,128)(2,1)} %get-tuple-element.199), kind=kOutput, calls=%fused_computation.10 | convolution fusion | flops 4046454784 | bytes 16252928 | tf_op jit(solution)/shard_map/isd,isf->idf/dot_general | solution.py:31
  489.6 14.5 %reshape.346 = bf16[4,4,256,2,512]{4,3,2,1,0:T(2,128)(2,1)} reshape(bf16[4,1024,1024]{2,1,0:T(8,128)(2,1)} %convolution_convert_fusion) | data formatting | bytes 16777216 | tf_op jit(solution)/shard_map/reshape | solution.py:309
  504.1 8.9 copy.299
  526.4 11.8 %bitcast_convert_fusion.1 = bf16[1536,1024]{1,0:T(8,128)(2,1)} fusion(f32[4,480]{1,0:T(4,128)S(1)} %select_reduce_fusion, s32[4,1536]{1,0:T(4,128)S(1)} %fusion.35, bf16[4,480,512]{2,1,0:T(8,128)(2,1)S(1)} %copy-done.72, bf16[4,512,1024]{2,1,0:T(8,128)(2,1)} %all-gather.13.cloned.1.call-done), kind=kOutput, calls=%fused_computation.12 | convolution fusion | flops 8061517824 | bytes 9338368 | tf_op jit(solution)/shard_map/ist,isd->td/dot_general | solution.py:31
  545.1 66.6 %all-to-all-done.11 = bf16[4,8,256,512]{3,2,1,0:T(8,128)(2,1)} async-done(((bf16[4,8,256,512]{3,2,1,0:T(8,128)(2,1)}), bf16[4,8,256,512]{3,2,1,0:T(8,128)(2,1)}, u32[]{:S(2)}, u32[]{:S(2)}) %all-to-all-start.11) | async-done | bytes 8388640 | tf_op jit(solution)/shard_map/all_to_all | solution.py:97
  620.1 6.7 reduce_sum.214
  645.3 79.1 %all-to-all-done.4 = bf16[8,768,256]{2,1,0:T(8,128)(2,1)} async-done(((bf16[8,768,256]{2,1,0:T(8,128)(2,1)}), bf16[8,768,256]{2,1,0:T(8,128)(2,1)}, u32[]{:S(2)}, u32[]{:S(2)}) %all-to-all-start.4) | async-done | bytes 3145760 | tf_op jit(solution)/shard_map/all_to_all | solution.py:60
  755.2 29.9 %all-to-all-done.12 = bf16[8,1,256,512]{3,2,1,0:T(8,128)(2,1)} async-done(((bf16[8,1,256,512]{3,2,1,0:T(8,128)(2,1)}), bf16[8,1,256,512]{3,2,1,0:T(8,128)(2,1)}, u32[]{:S(2)}, u32[]{:S(2)}) %all-to-all-start.12) | async-done | bytes 2097184 | tf_op jit(solution)/shard_map/all_to_all | solution.py:60
  798.1 11.3 %all-to-all-done.6 = bf16[8,192,256]{2,1,0:T(8,128)(2,1)} async-done(((bf16[8,192,256]{2,1,0:T(8,128)(2,1)}), bf16[8,192,256]{2,1,0:T(8,128)(2,1)}, u32[]{:S(2)}, u32[]{:S(2)}) %all-to-all-start.6) | async-done | bytes 786464 | tf_op jit(solution)/shard_map/all_to_all | solution.py:60
  847.3 6.2 multiply_subtract_fusion.1
  875.3 17.9 %multiply_subtract_fusion = (f32[8,256,2,256]{3,2,1,0:T(2,128)}, f32[8,256,2,256]{3,2,1,0:T(2,128)}, f32[8,256,2,256]{3,2,1,0:T(2,128)}) fusion(f32[8,256,2,256]{3,2,1,0:T(2,128)} %param.40, f32[8,256,2,256]{3,2,1,0:T(2,128)} %reshape.350, f32[8,256,2,256]{3,2,1,0:T(2,128)} %param.42, f32[8,256,2,256]{3,2,1,0:T(2,128)} %param.41), kind=kLoop, calls=%fused_computation.31 | loop fusion | flops 14680064 | bytes 29360128 | tf_op jit(solution)/shard_map/sub | solution.py:149
  893.8 18.3 %all-to-all-done.10 = bf16[4,4,256,384]{3,2,1,0:T(8,128)(2,1)S(1)} async-done(((bf16[4,4,256,384]{3,2,1,0:T(8,128)(2,1)}), bf16[4,4,256,384]{3,2,1,0:T(8,128)(2,1)S(1)}, u32[]{:S(2)}, u32[]{:S(2)}) %all-to-all-start.10) | async-done | bytes 3145760 | tf_op jit(solution)/shard_map/all_to_all | solution.py:48
  (345 shorter events, 295.8 us)
Async XLA Ops:
  8.5 11.9 %all-to-all-start.1 = ((f32[4,2,256]{2,1,0:T(2,128)}), f32[4,2,256]{2,1,0:T(2,128)S(1)}, u32[]{:S(2)}, u32[]{:S(2)}) async-start(f32[4,2,256]{2,1,0:T(2,128)} %broadcast_in_dim.79), calls=%async_computation.1 | async-start | bytes 16384 | tf_op jit(solution)/shard_map/all_to_all | solution.py:48
  20.4 17.1 %all-to-all-start.2 = ((bf16[4,256,256]{1,2,0:T(8,128)(2,1)}), bf16[4,256,256]{1,2,0:T(8,128)(2,1)S(1)}, u32[]{:S(2)}, u32[]{:S(2)}) async-start(bf16[4,256,256]{1,2,0:T(8,128)(2,1)} %maximum_bitcast_fusion.1), calls=%async_computation.2 | async-start | bytes 1048576 | tf_op jit(solution)/shard_map/all_to_all | solution.py:64
  23.9 119.5 %all-gather.17.cloned.1.call-start = ((), (), s32[]{:S(2)}) async-start(), calls=%async_computation.21 | async-start | bytes 3538944 | tf_op jit(solution)/shard_map/all_gather | solution.py:68
  37.5 111.0 %all-to-all-start = ((bf16[8,1,256,768]{3,2,1,0:T(8,128)(2,1)}), bf16[8,1,256,768]{3,2,1,0:T(8,128)(2,1)}, u32[]{:S(2)}, u32[]{:S(2)}) async-start(bf16[8,1,256,768]{3,2,1,0:T(8,128)(2,1)} %pad_maximum_fusion.3), calls=%async_computation | async-start | bytes 6291456 | tf_op jit(solution)/shard_map/all_to_all | solution.py:60
  42.4 316.3 %all-gather.9.cloned.1.call-start = ((), (), s32[]{:S(2)}) async-start(), calls=%async_computation.16 | async-start | bytes 3538944 | tf_op jit(solution)/shard_map/all_gather | solution.py:265
  43.7 122.8 %copy-start.17 = (pred[384,768]{1,0:T(8,128)(4,1)}, pred[384,768]{1,0:T(8,128)(4,1)S(1)}, u32[]{:S(2)}) copy-start(pred[384,768]{1,0:T(8,128)(4,1)S(1)} %compare_and_fusion.1) | copy-start | bytes 884740
  46.4 111.0 %copy-start.62 = (f32[1,4,256]{2,0,1:T(1,128)}, f32[1,4,256]{2,0,1:T(1,128)S(1)}, u32[]{:S(2)}) copy-start(f32[1,4,256]{2,0,1:T(1,128)S(1)} %get-tuple-element.210) | copy-start | bytes 12292
  170.0 206.9 %all-gather.11.cloned.1.call-start = ((), (), s32[]{:S(2)}) async-start(), calls=%async_computation.17 | async-start | bytes 10485760 | tf_op jit(solution)/shard_map/all_gather | solution.py:229
  172.7 90.1 %copy-start.49 = (bf16[768,256]{1,0:T(8,128)(2,1)S(1)}, bf16[768,256]{1,0:T(8,128)(2,1)}, u32[]{:S(2)}) copy-start(bf16[768,256]{1,0:T(8,128)(2,1)} %param.24) | copy-start | bytes 1179652
  264.7 74.5 %all-to-all-start.5 = ((bf16[8,768,256]{2,1,0:T(8,128)(2,1)}), bf16[8,768,256]{2,1,0:T(8,128)(2,1)S(1)}, u32[]{:S(2)}, u32[]{:S(2)}) async-start(bf16[8,768,256]{2,1,0:T(8,128)(2,1)} %broadcast_in_dim.151), calls=%async_computation.5 | async-start | bytes 6291456 | tf_op jit(solution)/shard_map/all_to_all | solution.py:48
  268.3 119.9 %all-gather.13.cloned.1.call-start = ((), (), s32[]{:S(2)}) async-start(), calls=%async_computation.18 | async-start | bytes 5242880 | tf_op jit(solution)/shard_map/all_gather | solution.py:230
  416.5 53.1 %all-to-all-start.13 = ((bf16[4,8,256,256]{3,2,1,0:T(8,128)(2,1)}), bf16[4,8,256,256]{3,2,1,0:T(8,128)(2,1)}, u32[]{:S(2)}, u32[]{:S(2)}) async-start(bf16[4,8,256,256]{3,2,1,0:T(8,128)(2,1)} %bitcast.256), calls=%async_computation.14 | async-start | bytes 8388608 | tf_op jit(solution)/shard_map/all_to_all | solution.py:97
  421.4 100.9 %reduce-scatter.2.cloned.1.call-start = ((), (), s32[]{:S(2)}) async-start(), calls=%async_computation.19 | async-start | bytes 3538944 | tf_op jit(solution)/shard_map/reduce_scatter | solution.py:76
  473.8 39.2 %all-to-all-start.14 = ((bf16[8,1,256,256]{3,2,1,0:T(8,128)(2,1)}), bf16[8,1,256,256]{3,2,1,0:T(8,128)(2,1)}, u32[]{:S(2)}, u32[]{:S(2)}) async-start(bf16[8,1,256,256]{3,2,1,0:T(8,128)(2,1)} %bitcast.267), calls=%async_computation.15 | async-start | bytes 2097152 | tf_op jit(solution)/shard_map/all_to_all | solution.py:60
  512.9 98.8 %all-to-all-start.11 = ((bf16[4,8,256,512]{3,2,1,0:T(8,128)(2,1)}), bf16[4,8,256,512]{3,2,1,0:T(8,128)(2,1)}, u32[]{:S(2)}, u32[]{:S(2)}) async-start(bf16[4,8,256,512]{3,2,1,0:T(8,128)(2,1)} %bitcast.249), calls=%async_computation.12 | async-start | bytes 16777216 | tf_op jit(solution)/shard_map/all_to_all | solution.py:97
  518.6 108.2 %all-gather.15.cloned.1.call-start = ((), (), s32[]{:S(2)}) async-start(), calls=%async_computation.20 | async-start | bytes 3538944 | tf_op jit(solution)/shard_map/all_gather | solution.py:330
  611.7 112.6 %all-to-all-start.4 = ((bf16[8,768,256]{2,1,0:T(8,128)(2,1)}), bf16[8,768,256]{2,1,0:T(8,128)(2,1)}, u32[]{:S(2)}, u32[]{:S(2)}) async-start(bf16[8,768,256]{2,1,0:T(8,128)(2,1)} %bitcast.37), calls=%async_computation.4 | async-start | bytes 6291456 | tf_op jit(solution)/shard_map/all_to_all | solution.py:60
  617.8 207.4 %all-gather.19.cloned.1.call-start = ((), (), s32[]{:S(2)}) async-start(), calls=%async_computation.22 | async-start | bytes 4718592 | tf_op jit(solution)/shard_map/all_gather | solution.py:333
  724.3 60.7 %all-to-all-start.12 = ((bf16[8,1,256,512]{3,2,1,0:T(8,128)(2,1)}), bf16[8,1,256,512]{3,2,1,0:T(8,128)(2,1)}, u32[]{:S(2)}, u32[]{:S(2)}) async-start(bf16[8,1,256,512]{3,2,1,0:T(8,128)(2,1)} %bitcast.263), calls=%async_computation.13 | async-start | bytes 4194304 | tf_op jit(solution)/shard_map/all_to_all | solution.py:60
  785.0 24.3 %all-to-all-start.6 = ((bf16[8,192,256]{2,1,0:T(8,128)(2,1)}), bf16[8,192,256]{2,1,0:T(8,128)(2,1)}, u32[]{:S(2)}, u32[]{:S(2)}) async-start(bf16[8,192,256]{2,1,0:T(8,128)(2,1)} %pad_maximum_fusion.4), calls=%async_computation.7 | async-start | bytes 1572864 | tf_op jit(solution)/shard_map/all_to_all | solution.py:60
  809.4 22.2 %all-to-all-start.9 = ((bf16[4,256,384]{2,1,0:T(8,128)(2,1)}), bf16[4,256,384]{2,1,0:T(8,128)(2,1)}, u32[]{:S(2)}, u32[]{:S(2)}) async-start(bf16[4,256,384]{2,1,0:T(8,128)(2,1)} %pad_maximum_fusion.5), calls=%async_computation.10 | async-start | bytes 1572864 | tf_op jit(solution)/shard_map/all_to_all | solution.py:64
  832.2 11.3 %all-to-all-start.8 = ((f32[32,2,256]{2,1,0:T(2,128)}), f32[32,2,256]{2,1,0:T(2,128)S(1)}, u32[]{:S(2)}, u32[]{:S(2)}) async-start(f32[32,2,256]{2,1,0:T(2,128)} %bitcast.68), calls=%async_computation.9 | async-start | bytes 131072 | tf_op jit(solution)/shard_map/all_to_all | solution.py:367
  843.6 24.4 %all-to-all-start.7 = ((f32[4,192,256]{2,1,0:T(8,128)}), f32[4,192,256]{2,1,0:T(8,128)S(1)}, u32[]{:S(2)}, u32[]{:S(2)}) async-start(f32[4,192,256]{2,1,0:T(8,128)} %bitcast.273), calls=%async_computation.8 | async-start | bytes 1572864 | tf_op jit(solution)/shard_map/all_to_all | solution.py:64
  871.5 40.6 %all-to-all-start.10 = ((bf16[4,4,256,384]{3,2,1,0:T(8,128)(2,1)}), bf16[4,4,256,384]{3,2,1,0:T(8,128)(2,1)S(1)}, u32[]{:S(2)}, u32[]{:S(2)}) async-start(bf16[4,4,256,384]{3,2,1,0:T(8,128)(2,1)} %broadcast_in_dim.153), calls=%async_computation.11 | async-start | bytes 6291456 | tf_op jit(solution)/shard_map/all_to_all | solution.py:48
  (75 other events, 663.4 us)
Sparse Core Ops, SparseCore 0:
  26.8 116.4 all-gather.16
  170.1 92.8 all-gather.8
  265.2 56.3 all-gather.10
  323.0 34.4 all-gather.12
  441.2 80.9 reduce-scatter.1
  526.5 61.4 all-gather.14
  621.3 131.8 all-gather.18

commit v3 on v2

--- a/solution.py
+++ b/solution.py
@@ -90,13 +90,15 @@
     return grid_exchange(split).swapaxes(0, 1), False
 
 
-def expert_blocks(grads, experts_here):
+def expert_blocks(grads, experts_here, reduced):
     grid = grads.shape[1]
     if experts_here % grid == 0:
-        dp_count = lax.axis_size("dp")
-        parts = lax.all_to_all(grads, "dp", split_axis=0, concat_axis=0, tiled=True)
-        parts = parts.reshape(dp_count, -1, *grads.shape[1:])
-        mine = low(jnp.sum(parts.astype(jnp.float32), axis=0))
+        if reduced:
+            mine = lax.psum_scatter(grads, "dp", scatter_dimension=0, tiled=True)
+        else:
+            parts = lax.all_to_all(grads, "dp", split_axis=0, concat_axis=0, tiled=True)
+            parts = parts.reshape(lax.axis_size("dp"), -1, *grads.shape[1:])
+            mine = low(jnp.sum(parts.astype(jnp.float32), axis=0))
         mine = grid_exchange(mine.swapaxes(0, 1)).swapaxes(0, 1)
         return mine.reshape(experts_here, *grads.shape[2:])
     every = grid_exchange(grads.swapaxes(0, 1)).swapaxes(0, 1)
@@ -228,7 +230,7 @@
     if spread:
         gate_up_mine = lax.all_gather(gate_up_mine, "dp", axis=0, tiled=True)
         down_mine = lax.all_gather(down_mine, "dp", axis=0, tiled=True)
-    cotangent_all = grid_whole(cotangent, copied)
+    cotangent_all = grid_whole(cotangent, gathered)
     gains_all = copies(norm_gains, ("col",)).transpose(1, 0, 2).reshape(2, MODEL_WIDTH)
 
     own_ids = jnp.arange(own_count, dtype=jnp.int32) * grid + place
@@ -268,6 +270,13 @@
     normed_two = low(middle * second_scale * gains_all[1])
 
     slot_inputs = low(product("ist,td->isd", pick, normed_two))
+    weight_in_here, slot_inputs = lax.optimization_barrier((weight_in_here, slot_inputs))
+    weight_in_all = lax.all_gather(weight_in_here, grid_axes, axis=0, tiled=False)
+    weight_in_all = (
+        weight_in_all.reshape(row_count, col_count, heads_here, width_part, head_width)
+        .transpose(0, 2, 1, 3, 4)
+        .reshape(grid, MODEL_WIDTH, head_width)
+    )
     gate_up = product("isd,idf->isf", slot_inputs, gate_up_mine)
     gate_part = jnp.concatenate(
         [gate_up[..., 2 * r * ff_part : (2 * r + 1) * ff_part] for r in range(row_count)], axis=2
@@ -279,12 +288,7 @@
     hidden = low(jax.nn.silu(gate_part) * up_part)
     expert_out = low(product("isf,ifd->isd", hidden, down_mine) * slot_weights)
     mixture = low(product("ist,isd->td", pick, expert_out))
-    mixture = grid_exchange(grid_split(mixture))
-    mixture = jnp.sum(mixture.astype(jnp.float32), axis=0)
-    middle_here = lax.dynamic_slice(
-        middle, (row_index * half_tokens, col_index * width_part), (half_tokens, width_part)
-    )
-    block_output = low(middle_here + mixture)
+    mixture = grid_split(mixture).reshape(-1, width_part)
 
     grad_slots = low(product("ist,td->isd", pick, cotangent_all) * slot_weights)
     grad_hidden = product("isd,ifd->isf", grad_slots, down_mine)
@@ -314,9 +318,7 @@
         own_count, row_count, ff_part, col_count, width_part
     ).transpose(0, 1, 3, 2, 4)
     down_grads = down_grads.reshape(own_count, grid, ff_part, width_part)
-    grad_gate_up = expert_blocks(gate_up_grads, experts_here).astype(jnp.float32)
-    grad_gate_up = grad_gate_up.reshape(gate_up_weight.shape)
-    grad_down = expert_blocks(down_grads, experts_here).astype(jnp.float32)
+    grad_down = expert_blocks(down_grads, experts_here, False).astype(jnp.float32)
 
     middle_part = own_rows(middle, place, part_tokens)
     scale_part = own_rows(second_scale, place, part_tokens)
@@ -329,13 +331,17 @@
     grad_gain_two = jnp.sum(grad_normed_two * middle_part * scale_part, axis=0)
     grad_middle_all = lax.all_gather(low(grad_middle), grid_axes, axis=0, tiled=True)
 
-    weight_in_here, grad_middle = lax.optimization_barrier((weight_in_here, grad_middle))
-    weight_in_all = lax.all_gather(weight_in_here, grid_axes, axis=0, tiled=False)
-    weight_in_all = (
-        weight_in_all.reshape(row_count, col_count, heads_here, width_part, head_width)
-        .transpose(0, 2, 1, 3, 4)
-        .reshape(grid, MODEL_WIDTH, head_width)
-    )
+    gate_up_grads, mixture, grad_middle_all = lax.optimization_barrier(
+        (gate_up_grads, mixture, grad_middle_all)
+    )
+    grad_gate_up = expert_blocks(gate_up_grads, experts_here, True).astype(jnp.float32)
+    grad_gate_up = grad_gate_up.reshape(gate_up_weight.shape)
+    mixture = grid_total(mixture).astype(jnp.float32)
+    middle_here = lax.dynamic_slice(
+        middle, (row_index * half_tokens, col_index * width_part), (half_tokens, width_part)
+    )
+    block_output = low(middle_here + mixture)
+
     out_mine = own_rows(out_all, place, head_span)
     grad_context = low(product("td,hd->th", grad_middle_all, out_mine))
     out_grads = product("th,td->hd", context, grad_middle_all)

time: 949 us -> 903 us (0.952)
  blocking collectives: 89.9 us -> 39.4 us
  waiting for transfers between devices: 402 us -> 438 us
  starting transfers between devices: 64.5 us -> 48.6 us
    all_gather x1 -> x2, waiting for transfers between devices: 95.9 us -> 0.02 us  [gathered(): return lax.all_gather(block, grid_axes, axis=0, tiled=False)]
    reduce_scatter x1 -> x2, waiting for transfers between devices: 1.07 us -> 71.9 us  [grid_total(): return lax.psum_scatter(blocks, grid_axes, scatter_dimension=0, tiled=True)]
    all_to_all x1, blocking collectives: 89.9 us -> 39.4 us  [copies(): return lax.all_to_all(equal, axes, split_axis=0, concat_axis=0, tiled=True)]
    all_to_all x2 -> x1, waiting for transfers between devices: 95.1 us -> 48.2 us  [expert_blocks(): parts = lax.all_to_all(grads, 'dp', split_axis=0, concat_axis=0, tiled=True)]
    all_to_all x3, waiting for transfers between devices: 5.82 us -> 50.8 us  [col_exchange(): lax.all_to_all(blocks, 'col', split_axis=0, concat_axis=0, tiled=True)]
    all_gather x1, waiting for transfers between devices: 0.01 us -> 40.4 us  [per_device(): gate_up_mine = lax.all_gather(gate_up_mine, 'dp', axis=0, tiled=True)]
    all_gather x1, waiting for transfers between devices: 0.01 us -> 24.2 us  [per_device(): down_mine = lax.all_gather(down_mine, 'dp', axis=0, tiled=True)]
    all_to_all x3 -> x2, waiting for transfers between devices: 78.6 us -> 64.1 us  [copies(): return lax.all_to_all(equal, axes, split_axis=0, concat_axis=0, tiled=True)]
  transfers between devices with their start and end apart: 21 -> 21, of which waited for: 14 -> 15; matrix products, arithmetic and copies ran while one was open for 30% -> 32% of each run, Pallas kernels for 0% -> 0%
where the time goes in v3:
time: 903 us; the launch traced here: 896 us
  waiting for transfers between devices  438 us (49%)
  local copies, waits for them, and re-layouts  152 us (17%)
  matrix products  126 us (14%)
  other arithmetic  75.2 us (8%)
  starting transfers between devices  48.6 us (5%)
  blocking collectives  39.4 us (4%)
  between operations  15.8 us (2%)
    dot_general x39, matrix products, product(): return jnp.einsum(formula, left, right, preferred_element_type=jnp.float32)  126 us
    all_to_all x4, waiting for transfers between devices, grid_exchange(): lax.all_to_all(blocks, grid_axes, split_axis=0, concat_axis=0, tiled=True)  114 us
    reduce_scatter x2, waiting for transfers between devices, grid_total(): return lax.psum_scatter(blocks, grid_axes, scatter_dimension=0, tiled=True)  71.9 us
    all_to_all x2, waiting for transfers between devices, copies(): return lax.all_to_all(equal, axes, split_axis=0, concat_axis=0, tiled=True)  64.1 us
    all_to_all x3, waiting for transfers between devices, col_exchange(): lax.all_to_all(blocks, 'col', split_axis=0, concat_axis=0, tiled=True)  50.8 us
    all_to_all x1, waiting for transfers between devices, expert_blocks(): parts = lax.all_to_all(grads, 'dp', split_axis=0, concat_axis=0, tiled=True)  48.2 us
    unnamed x190, local copies, waits for them, and re-layouts  41.6 us
    all_gather x1, waiting for transfers between devices, per_device(): gate_up_mine = lax.all_gather(gate_up_mine, 'dp', axis=0, tiled=True)  40.4 us
  transfers between devices with their start and end apart: 21, of which 15 were waited for; matrix products, arithmetic and copies ran while one was open for 32% of the time, Pallas kernels for 0%

profile of v3, /device:TPU:0, one launch (start us, length us, event | category | flops | bytes accessed | tf_op | source)
XLA Modules:
  0.0 895.6 jit_solution(6906381805089909544)
XLA Ops:
  36.6 12.1 %all-to-all-done.2 = bf16[4,256,256]{1,2,0:T(8,128)(2,1)S(1)} async-done(((bf16[4,256,256]{1,2,0:T(8,128)(2,1)}), bf16[4,256,256]{1,2,0:T(8,128)(2,1)S(1)}, u32[]{:S(2)}, u32[]{:S(2)}) %all-to-all-start.2) | async-done | bytes 524320 | tf_op jit(solution)/shard_map/all_to_all | solution.py:64
  60.0 89.3 %all-to-all-done = bf16[8,1,256,768]{3,2,1,0:T(8,128)(2,1)S(1)} async-done(((bf16[8,1,256,768]{3,2,1,0:T(8,128)(2,1)}), bf16[8,1,256,768]{3,2,1,0:T(8,128)(2,1)S(1)}, u32[]{:S(2)}, u32[]{:S(2)}) %all-to-all-start) | async-done | bytes 3145760 | tf_op jit(solution)/shard_map/all_to_all | solution.py:60
  188.8 62.8 %all-to-all-done.3 = bf16[8,512,256]{2,1,0:T(8,128)(2,1)} async-done(((bf16[8,512,256]{2,1,0:T(8,128)(2,1)}), bf16[8,512,256]{2,1,0:T(8,128)(2,1)}, u32[]{:S(2)}, u32[]{:S(2)}) %all-to-all-start.3) | async-done | bytes 2097184 | tf_op jit(solution)/shard_map/all_to_all | solution.py:48
  265.6 9.6 %multiply_convert_fusion.1 = bf16[4,480,1024]{2,1,0:T(8,128)(2,1)} fusion(f32[4,480]{1,0:T(4,128)S(1)} %select_reduce_fusion, bf16[1536,1024,1]{1,0,2:T(8,128)(2,1)} %reshape.359, s32[4,1536]{1,0:T(4,128)S(1)} %fusion.35), kind=kOutput, calls=%fused_computation.9 | convolution fusion | flops 6046679040 | bytes 7110144 | tf_op jit(solution)/shard_map/ist,td->isd/dot_general | solution.py:31
  275.3 13.4 %all-gather.11.cloned.1.call-done = bf16[1536,1024]{0,1:T(8,128)(2,1)} async-done(((bf16[1536,128]{0,1:T(8,128)(2,1)}), bf16[1536,1024]{0,1:T(8,128)(2,1)}) %all-gather.11.cloned.1.call-update) | async-done | bytes 3145744 | tf_op jit(solution)/shard_map/all_gather | solution.py:267
  299.1 8.1 fusion.25
  307.2 40.4 %all-gather.15.cloned.1.call-done = bf16[4,1024,1024]{2,1,0:T(8,128)(2,1)} async-done(((bf16[1,1024,1024]{2,1,0:T(8,128)(2,1)}), bf16[4,1024,1024]{2,1,0:T(8,128)(2,1)}) %all-gather.15.cloned.1.call-update) | async-done | bytes 8388624 | tf_op jit(solution)/shard_map/all_gather | solution.py:231
  347.6 8.0 fusion.117
  359.3 24.2 %all-gather.13.cloned.1.call-done = bf16[4,512,1024]{2,1,0:T(8,128)(2,1)} async-done(((bf16[1,512,1024]{2,1,0:T(8,128)(2,1)}), bf16[4,512,1024]{2,1,0:T(8,128)(2,1)}) %all-gather.13.cloned.1.call-update) | async-done | bytes 4194320 | tf_op jit(solution)/shard_map/all_gather | solution.py:232
  383.5 9.1 %multiply_convert_fusion.6 = (bf16[4,480,512]{2,1,0:T(8,128)(2,1)}, bf16[4,480,512]{2,1,0:T(8,128)(2,1)S(1)}, bf16[4,480,512]{2,1,0:T(8,128)(2,1)S(1)}) fusion(f32[4,480,256]{2,1,0:T(8,128)} %get-tuple-element.202, f32[4,480,256]{2,1,0:T(8,128)} %get-tuple-element.199, f32[4,480,256]{2,1,0:T(8,128)} %get-tuple-element.200, ...), kind=kOutput, calls=%fused_computation.39 | convolution fusion | flops 2030960640 | bytes 21889024 | tf_op jit(solution)/shard_map/isd,ifd->isf/dot_general | solution.py:31
  394.6 15.6 %bitcast_convert_fusion = bf16[1536,1024]{1,0:T(8,128)(2,1)} fusion(bf16[4,1024,1024]{2,1,0:T(8,128)(2,1)} %all-gather.15.cloned.1.call-done, s32[4,1536]{1,0:T(4,128)S(1)} %fusion.35, bf16[4,480,256]{2,1,0:T(8,128)(2,1)} %get-tuple-element.240, bf16[4,480,256]{2,1,0:T(8,128)(2,1)} %get-tuple-element.206, bf16[4,480,256]{2,1,0:T(8,128)(2,1)} %get-tuple-element.241, ...), kind=kOutput, calls=%fused_computation.11 | convolution fusion | flops 10088546304 | bytes 15491072 | tf_op jit(solution)/shard_map/ist,isd->td/dot_general | solution.py:31
  412.8 71.9 %reduce-scatter.4.cloned.1.call-done = bf16[192,1024]{1,0:T(8,128)(2,1)} async-done(((bf16[1536,1024]{1,0:T(8,128)(2,1)}), bf16[192,1024]{1,0:T(8,128)(2,1)}) %reduce-scatter.4.cloned.1.call-update) | async-done | bytes 393232 | tf_op jit(solution)/shard_map/reduce_scatter | solution.py:76
  491.4 10.3 %convolution_convert_fusion = bf16[4,1024,1024]{2,1,0:T(8,128)(2,1)} fusion(bf16[4,480,1024]{2,1,0:T(8,128)(2,1)} %fusion.25, bf16[4,480,256]{2,1,0:T(8,128)(2,1)S(1)} %copy-done.43, bf16[4,480,256]{2,1,0:T(8,128)(2,1)S(1)} %copy-done.42, bf16[4,480,256]{2,1,0:T(8,128)(2,1)} %get-tuple-element.241, bf16[4,480,256]{2,1,0:T(8,128)(2,1)S(1)} %copy-done.41), kind=kOutput, calls=%fused_computation.10 | convolution fusion | flops 4046454784 | bytes 16252928 | tf_op jit(solution)/shard_map/isd,isf->idf/dot_general | solution.py:31
  501.8 14.9 %reshape.325 = bf16[4,4,256,2,512]{4,3,2,1,0:T(2,128)(2,1)} reshape(bf16[4,1024,1024]{2,1,0:T(8,128)(2,1)} %convolution_convert_fusion) | data formatting | bytes 16777216 | tf_op jit(solution)/shard_map/reshape | solution.py:313
  516.7 9.2 %copy.282 = bf16[4,4,256,2,512]{4,2,1,3,0:T(8,128)(2,1)} copy(bf16[4,4,256,2,512]{4,3,2,1,0:T(2,128)(2,1)} %reshape.325) | data formatting | bytes 16777216 | tf_op jit(solution)/shard_map/reshape | solution.py:313
  525.8 11.8 %bitcast_convert_fusion.1 = bf16[1536,1024]{1,0:T(8,128)(2,1)} fusion(f32[4,480]{1,0:T(4,128)S(1)} %select_reduce_fusion, s32[4,1536]{1,0:T(4,128)S(1)} %fusion.35, bf16[4,480,512]{2,1,0:T(8,128)(2,1)S(1)} %copy-done.81, bf16[4,512,1024]{2,1,0:T(8,128)(2,1)} %all-gather.13.cloned.1.call-done), kind=kOutput, calls=%fused_computation.12 | convolution fusion | flops 8061517824 | bytes 9338368 | tf_op jit(solution)/shard_map/ist,isd->td/dot_general | solution.py:31
  557.2 7.9 reshape.340
  574.9 48.2 %all-to-all-done.10 = bf16[4,8,256,256]{3,2,1,0:T(8,128)(2,1)} async-done(((bf16[4,8,256,256]{3,2,1,0:T(8,128)(2,1)}), bf16[4,8,256,256]{3,2,1,0:T(8,128)(2,1)}, u32[]{:S(2)}, u32[]{:S(2)}) %all-to-all-start.10) | async-done | bytes 4194336 | tf_op jit(solution)/shard_map/all_to_all | solution.py:99
  686.2 12.2 %all-to-all-done.4 = bf16[8,192,256]{2,1,0:T(8,128)(2,1)} async-done(((bf16[8,192,256]{2,1,0:T(8,128)(2,1)}), bf16[8,192,256]{2,1,0:T(8,128)(2,1)}, u32[]{:S(2)}, u32[]{:S(2)}) %all-to-all-start.4) | async-done | bytes 786464 | tf_op jit(solution)/shard_map/all_to_all | solution.py:60
  711.7 9.7 %all-to-all-done.7 = bf16[4,256,384]{2,1,0:T(8,128)(2,1)} async-done(((bf16[4,256,384]{2,1,0:T(8,128)(2,1)}), bf16[4,256,384]{2,1,0:T(8,128)(2,1)}, u32[]{:S(2)}, u32[]{:S(2)}) %all-to-all-start.7) | async-done | bytes 786464 | tf_op jit(solution)/shard_map/all_to_all | solution.py:64
  736.0 29.0 %all-to-all-done.5 = f32[4,192,256]{2,1,0:T(8,128)S(1)} async-done(((f32[4,192,256]{2,1,0:T(8,128)}), f32[4,192,256]{2,1,0:T(8,128)S(1)}, u32[]{:S(2)}, u32[]{:S(2)}) %all-to-all-start.5) | async-done | bytes 786464 | tf_op jit(solution)/shard_map/all_to_all | solution.py:64
  767.5 39.4 %all_to_all.60 = bf16[4,4,256,384]{3,2,1,0:T(8,128)(2,1)S(1)} all-to-all(bf16[4,4,256,384]{3,2,1,0:T(8,128)(2,1)S(1)} %broadcast_in_dim.146), channel_id=1, replica_groups=mesh['dp'=4,'row'=2,'col'=4] {'dp'}, dimensions={0} | all-to-all | bytes 6291456 | tf_op jit(solution)/shard_map/all_to_all | solution.py:48
  851.8 12.5 %all-to-all-done.9 = bf16[8,1,256,512]{3,2,1,0:T(8,128)(2,1)} async-done(((bf16[8,1,256,512]{3,2,1,0:T(8,128)(2,1)}), bf16[8,1,256,512]{3,2,1,0:T(8,128)(2,1)}, u32[]{:S(2)}, u32[]{:S(2)}) %all-to-all-start.9) | async-done | bytes 2097184 | tf_op jit(solution)/shard_map/all_to_all | solution.py:60
  869.7 17.9 %multiply_subtract_fusion = (f32[8,256,2,256]{3,2,1,0:T(2,128)}, f32[8,256,2,256]{3,2,1,0:T(2,128)}, f32[8,256,2,256]{3,2,1,0:T(2,128)}) fusion(f32[8,256,2,256]{3,2,1,0:T(2,128)} %param.40, f32[8,256,2,256]{3,2,1,0:T(2,128)} %reshape.342, f32[8,256,2,256]{3,2,1,0:T(2,128)} %param.42, f32[8,256,2,256]{3,2,1,0:T(2,128)} %param.41), kind=kLoop, calls=%fused_computation.30 | loop fusion | flops 14680064 | bytes 29360128 | tf_op jit(solution)/shard_map/sub | solution.py:151
  (365 shorter events, 292.3 us)
Async XLA Ops:
  7.2 147.7 %all-gather.19.cloned.1.call-start = ((), (), s32[]{:S(2)}) async-start(), calls=%async_computation.22 | async-start | bytes 3538944 | tf_op jit(solution)/shard_map/all_gather | solution.py:68
  9.2 11.9 %all-to-all-start.1 = ((f32[4,2,256]{2,1,0:T(2,128)}), f32[4,2,256]{2,1,0:T(2,128)S(1)}, u32[]{:S(2)}, u32[]{:S(2)}) async-start(f32[4,2,256]{2,1,0:T(2,128)} %broadcast_in_dim.77), calls=%async_computation.1 | async-start | bytes 16384 | tf_op jit(solution)/shard_map/all_to_all | solution.py:48
  21.1 27.6 %all-to-all-start.2 = ((bf16[4,256,256]{1,2,0:T(8,128)(2,1)}), bf16[4,256,256]{1,2,0:T(8,128)(2,1)S(1)}, u32[]{:S(2)}, u32[]{:S(2)}) async-start(bf16[4,256,256]{1,2,0:T(8,128)(2,1)} %maximum_bitcast_fusion.1), calls=%async_computation.2 | async-start | bytes 1048576 | tf_op jit(solution)/shard_map/all_to_all | solution.py:64
  49.5 99.8 %all-to-all-start = ((bf16[8,1,256,768]{3,2,1,0:T(8,128)(2,1)}), bf16[8,1,256,768]{3,2,1,0:T(8,128)(2,1)S(1)}, u32[]{:S(2)}, u32[]{:S(2)}) async-start(bf16[8,1,256,768]{3,2,1,0:T(8,128)(2,1)} %pad_maximum_fusion.3), calls=%async_computation | async-start | bytes 6291456 | tf_op jit(solution)/shard_map/all_to_all | solution.py:60
  53.1 203.5 %all-gather.21.cloned.1.call-start = ((), (), s32[]{:S(2)}) async-start(), calls=%async_computation.23 | async-start | bytes 3538944 | tf_op jit(solution)/shard_map/all_gather | solution.py:68
  53.9 234.8 %all-gather.11.cloned.1.call-start = ((), (), s32[]{:S(2)}) async-start(), calls=%async_computation.15 | async-start | bytes 3538944 | tf_op jit(solution)/shard_map/all_gather | solution.py:267
  55.2 113.8 %copy-start.15 = (pred[384,768]{1,0:T(8,128)(4,1)}, pred[384,768]{1,0:T(8,128)(4,1)S(1)}, u32[]{:S(2)}) copy-start(pred[384,768]{1,0:T(8,128)(4,1)S(1)} %compare_and_fusion.1) | copy-start | bytes 884740
  57.9 102.8 %copy-start.69 = (f32[1,4,256]{2,0,1:T(1,128)}, f32[1,4,256]{2,0,1:T(1,128)S(1)}, u32[]{:S(2)}) copy-start(f32[1,4,256]{2,0,1:T(1,128)S(1)} %get-tuple-element.216) | copy-start | bytes 12292
  172.6 175.0 %all-gather.15.cloned.1.call-start = ((), (), s32[]{:S(2)}) async-start(), calls=%async_computation.17 | async-start | bytes 10485760 | tf_op jit(solution)/shard_map/all_gather | solution.py:231
  179.2 72.4 %all-to-all-start.3 = ((bf16[8,512,256]{2,1,0:T(8,128)(2,1)}), bf16[8,512,256]{2,1,0:T(8,128)(2,1)}, u32[]{:S(2)}, u32[]{:S(2)}) async-start(bf16[8,512,256]{2,1,0:T(8,128)(2,1)} %broadcast_in_dim.85), calls=%async_computation.3 | async-start | bytes 4194304 | tf_op jit(solution)/shard_map/all_to_all | solution.py:48
  183.5 200.0 %all-gather.13.cloned.1.call-start = ((), (), s32[]{:S(2)}) async-start(), calls=%async_computation.16 | async-start | bytes 5242880 | tf_op jit(solution)/shard_map/all_gather | solution.py:232
  186.1 298.6 %reduce-scatter.4.cloned.1.call-start = ((), (), s32[]{:S(2)}) async-start(), calls=%async_computation.18 | async-start | bytes 3538944 | tf_op jit(solution)/shard_map/reduce_scatter | solution.py:76
  410.3 138.9 %all-gather.17.cloned.1.call-start = ((), (), s32[]{:S(2)}) async-start(), calls=%async_computation.19 | async-start | bytes 3538944 | tf_op jit(solution)/shard_map/all_gather | solution.py:332
  412.8 88.9 %copy-start.67 = (f32[192]{0:T(256)}, f32[192]{0:T(256)S(1)}, u32[]{:S(2)}) copy-start(f32[192]{0:T(256)S(1)} %dynamic-slice.6) | copy-start | bytes 2308
  489.2 216.8 %all-gather.23.cloned.1.call-start = ((), (), s32[]{:S(2)}) async-start(), calls=%async_computation.24 | async-start | bytes 4718592 | tf_op jit(solution)/shard_map/all_gather | solution.py:274
  491.4 315.5 %reduce-scatter.8.cloned.1.call-start = ((), (), s32[]{:S(2)}) async-start(), calls=%async_computation.21 | async-start | bytes 10485760 | tf_op jit(solution)/shard_map/reduce_scatter | solution.py:97
  570.1 53.1 %all-to-all-start.10 = ((bf16[4,8,256,256]{3,2,1,0:T(8,128)(2,1)}), bf16[4,8,256,256]{3,2,1,0:T(8,128)(2,1)}, u32[]{:S(2)}, u32[]{:S(2)}) async-start(bf16[4,8,256,256]{3,2,1,0:T(8,128)(2,1)} %bitcast.259), calls=%async_computation.13 | async-start | bytes 8388608 | tf_op jit(solution)/shard_map/all_to_all | solution.py:99
  627.3 44.0 %all-to-all-start.11 = ((bf16[8,1,256,256]{3,2,1,0:T(8,128)(2,1)}), bf16[8,1,256,256]{3,2,1,0:T(8,128)(2,1)}, u32[]{:S(2)}, u32[]{:S(2)}) async-start(bf16[8,1,256,256]{3,2,1,0:T(8,128)(2,1)} %bitcast.88), calls=%async_computation.14 | async-start | bytes 2097152 | tf_op jit(solution)/shard_map/all_to_all | solution.py:60
  671.2 27.1 %all-to-all-start.4 = ((bf16[8,192,256]{2,1,0:T(8,128)(2,1)}), bf16[8,192,256]{2,1,0:T(8,128)(2,1)}, u32[]{:S(2)}, u32[]{:S(2)}) async-start(bf16[8,192,256]{2,1,0:T(8,128)(2,1)} %pad_maximum_fusion.4), calls=%async_computation.6 | async-start | bytes 1572864 | tf_op jit(solution)/shard_map/all_to_all | solution.py:60
  698.4 23.0 %all-to-all-start.7 = ((bf16[4,256,384]{2,1,0:T(8,128)(2,1)}), bf16[4,256,384]{2,1,0:T(8,128)(2,1)}, u32[]{:S(2)}, u32[]{:S(2)}) async-start(bf16[4,256,384]{2,1,0:T(8,128)(2,1)} %pad_maximum_fusion.5), calls=%async_computation.9 | async-start | bytes 1572864 | tf_op jit(solution)/shard_map/all_to_all | solution.py:64
  722.1 9.9 %all-to-all-start.6 = ((f32[32,2,256]{2,1,0:T(2,128)}), f32[32,2,256]{2,1,0:T(2,128)S(1)}, u32[]{:S(2)}, u32[]{:S(2)}) async-start(f32[32,2,256]{2,1,0:T(2,128)} %bitcast.70), calls=%async_computation.8 | async-start | bytes 131072 | tf_op jit(solution)/shard_map/all_to_all | solution.py:373
  731.9 33.1 %all-to-all-start.5 = ((f32[4,192,256]{2,1,0:T(8,128)}), f32[4,192,256]{2,1,0:T(8,128)S(1)}, u32[]{:S(2)}, u32[]{:S(2)}) async-start(f32[4,192,256]{2,1,0:T(8,128)} %bitcast.245), calls=%async_computation.7 | async-start | bytes 1572864 | tf_op jit(solution)/shard_map/all_to_all | solution.py:64
  735.4 114.3 %reduce-scatter.6.cloned.1.call-start = ((), (), s32[]{:S(2)}) async-start(), calls=%async_computation.20 | async-start | bytes 3538944 | tf_op jit(solution)/shard_map/reduce_scatter | solution.py:76
  806.9 57.4 %all-to-all-start.9 = ((bf16[8,1,256,512]{3,2,1,0:T(8,128)(2,1)}), bf16[8,1,256,512]{3,2,1,0:T(8,128)(2,1)}, u32[]{:S(2)}, u32[]{:S(2)}) async-start(bf16[8,1,256,512]{3,2,1,0:T(8,128)(2,1)} %bitcast.278), calls=%async_computation.12 | async-start | bytes 4194304 | tf_op jit(solution)/shard_map/all_to_all | solution.py:60
  (85 other events, 815.6 us)
Sparse Core Ops, SparseCore 0:
  10.1 125.8 all-gather.18
  138.1 64.4 all-gather.20
  205.2 83.3 all-gather.10
  290.7 56.8 all-gather.14
  349.0 34.4 all-gather.12
  410.4 74.2 reduce-scatter.3
  489.4 59.7 all-gather.16
  551.8 71.9 all-gather.22
  626.5 70.0 reduce-scatter.7
  740.0 81.2 reduce-scatter.5
